TPU v7x, 32 devices: a whole 2x2x4 slice. The times are simulated.
32 devices in a mesh: row: 4 (over z), col: 8 (over y, x, core).
Axes of the slice: x: 2, y: 2, z: 4, core: 2. Of those that a mesh axis runs over, the one named last changes fastest.
Arguments:
- tile_values: float32 [512, 512, 512], P(('row', 'col')), may hold values from -6 to 6
- tile_coords: int32 [512, 2], P(('row', 'col')), may hold values from 0 to 3, as said below
- tile_counts: int32 [32], P(('row', 'col')), may hold values from 4 to 16, as said below
- restrict_basis: float32 [8192, 256], P(('row', 'col')), may hold values from -0.25 to 0.25
- prolong_basis: float32 [16384, 256], P(('col', 'row')), may hold values from -0.25 to 0.25
- row_partner: int32 [8, 4], replicated, may hold values from 0 to 3, as said below
- col_partner: int32 [4, 8], replicated, may hold values from 0 to 7, as said below
Outputs:
- coarse: float32 [2048, 4096], P('row', 'col')
Inputs may be any that keep to these rules, and one draw needn't show every extreme that they name: `tile_coords`: within one device's 16 slots no two name the same (block row, block column); first entry below 4, second below 4; dead slots also hold such positions. `tile_counts`: number of leading slots of each device that are live; some device has all 16 live. `row_partner`: each row is a pairing: the partner of a part's partner is the part itself, never the part. `col_partner`: each row is a pairing: the partner of a part's partner is the part itself, never the part.
All inputs are finite; a program needn't handle non-finite values.
Results may differ from a plain program's by a relative error of at most 0.0003.
Values sent between devices are 32-bit elements; how exact they have to be, the bound alone decides.
No kernel may reach another device: no remote copies, remote signals or barrier semaphores. Data moves between devices by JAX's collectives and lax.ppermute only.
A program may use at most 128 MiB of HBM per device.

v0:
```python
import functools

import jax
import jax.numpy as jnp
from jax import lax
from jax.experimental import pallas as pl
from jax.experimental.pallas import tpu as pltpu
from jax.sharding import PartitionSpec as P

F32 = jnp.float32
BF16 = jnp.bfloat16
VMEM_BYTES = 48 * 1024 * 1024
PARAMS = pltpu.CompilerParams(vmem_limit_bytes=VMEM_BYTES)


def cost(flops):
    return pl.CostEstimate(flops=flops, bytes_accessed=0, transcendentals=0)


def split(value):
    high = value.astype(BF16)
    low = (value - high.astype(F32)).astype(BF16)
    return high, low


def dot(left, right):
    return jnp.dot(left, right, preferred_element_type=F32)


def product(left_both, right_high, right_low):
    half = left_both.shape[0] // 2
    total = dot(left_both[half:], right_high)
    total = total + dot(left_both[:half], right_low)
    return total + dot(left_both[:half], right_high)


def div(value, by):
    return lax.div(value, jnp.int32(by))


def rem(value, by):
    return lax.rem(value, jnp.int32(by))


def half_of(given, me, row_partner):
    mate = row_partner[me[0], me[1]]
    return ((mate > me[0]) if given else (me[0] > mate)).astype(jnp.int32)


def tables_kernel(block_cols, me, row_partner, col_partner, coords, counts, slots, first, wish):
    for place in range(slots.shape[0]):
        slots[place] = jnp.int32(-1)
    for slot in range(coords.shape[1]):

        @pl.when(slot < counts[0])
        def _():
            slots[coords[0, slot] * block_cols + coords[1, slot]] = jnp.int32(slot)

    first[0] = (me[0] ^ row_partner[me[0], me[1]]) - 1
    other = me[1] ^ 1
    wish[0] = div(other ^ col_partner[me[0], other], 2)


def make_tables(me, row_partner, col_partner, coords, counts, places, block_cols):
    smem = pl.BlockSpec(memory_space=pltpu.SMEM)
    return pl.pallas_call(
        functools.partial(tables_kernel, block_cols),
        in_specs=[smem] * 5,
        out_specs=[smem] * 3,
        out_shape=[jax.ShapeDtypeStruct((n,), jnp.int32) for n in (places, 1, 1)],
        cost_estimate=cost(0),
        name="make_tables",
    )(me, row_partner, col_partner, coords, counts)


class Columns:
    ON, REST, KEPT = range(3)

    def __init__(self, kind, block_cols):
        self.kind = kind
        self.given = kind != self.KEPT
        self.half_cols = block_cols // 2
        self.steps = block_cols if kind == self.KEPT else self.half_cols

    def half(self, step, me, row_partner, col_partner):
        if self.kind == self.KEPT:
            goes_on = (me[1] < col_partner[me[0], me[1]]).astype(jnp.int32)
            return goes_on ^ div(step, self.half_cols)
        goes_on = (me[1] < col_partner[row_partner[me[0], me[1]], me[1]]).astype(jnp.int32)
        return goes_on ^ (1 if self.kind == self.REST else 0)

    def column(self, step, me, row_partner, col_partner):
        half = self.half(step, me, row_partner, col_partner)
        return half * self.half_cols + rem(step, self.half_cols)


def left_kernel(columns, block_cols, half_rows, per_step, *refs):
    me, slots, row_partner, col_partner = refs[:4]
    tile_refs, q_refs, out, q_both = refs[4 : 4 + per_step], refs[4 + per_step : -2], refs[-2], refs[-1]
    group, step = pl.program_id(0), pl.program_id(1)
    width = q_both.shape[0] // 2

    block_row = half_of(columns.given, me, row_partner) * half_rows + group

    def put(value, first):
        high, low = split(value.T)
        q_both[:width, first : first + value.shape[0]] = high
        q_both[width:, first : first + value.shape[0]] = low

    if len(q_refs) == 1:

        @pl.when(step == 0)
        def _():
            put(q_refs[0][...], 0)

    else:
        distance = block_row ^ div(me[1], 2)
        for core in range(2):

            @pl.when((step == 0) & (rem(me[1], 2) == core))
            def _():
                depth = q_refs[0].shape[1]
                put(q_refs[0][distance], core * depth)
                put(q_refs[1][distance], (1 - core) * depth)

    for index, tile_ref in enumerate(tile_refs):
        column = columns.column(step * per_step + index, me, row_partner, col_partner)
        live = slots[block_row * block_cols + column] >= 0
        high, low = split(tile_ref[0])
        total = jnp.where(live, product(q_both[...], high, low), 0.0)
        out[index, 0], out[index, 1] = split(total)


def left_products(kind, tables, tiles, q_pieces, half_rows, block_cols):
    _, tile_order, _ = tiles.shape
    width = q_pieces[0].shape[-1]
    columns = Columns(kind, block_cols)
    per_step = 2 if columns.steps % 2 == 0 else 1

    def row_of(g, me, row_partner):
        return half_of(columns.given, me, row_partner) * half_rows + g

    def tile_spec(index):
        def tile_at(g, b, me, slots, row_partner, col_partner):
            column = columns.column(b * per_step + index, me, row_partner, col_partner)
            return jnp.maximum(slots[row_of(g, me, row_partner) * block_cols + column], 0), 0, 0

        return pl.BlockSpec((1, tile_order, tile_order), tile_at)

    if len(q_pieces) == 1:
        q_specs = [
            pl.BlockSpec(
                (tile_order, width),
                lambda g, b, me, slots, row_partner, _: (row_of(g, me, row_partner), 0),
            )
        ]
    else:
        q_specs = [pl.BlockSpec(memory_space=pltpu.VMEM)] * len(q_pieces)
    return pl.pallas_call(
        functools.partial(left_kernel, columns, block_cols, half_rows, per_step),
        grid_spec=pltpu.PrefetchScalarGridSpec(
            num_scalar_prefetch=4,
            grid=(half_rows, columns.steps // per_step),
            in_specs=[tile_spec(index) for index in range(per_step)] + q_specs,
            out_specs=pl.BlockSpec(
                (per_step, 2, width, tile_order), lambda g, b, *_: (b, 0, g, 0)
            ),
            scratch_shapes=[pltpu.VMEM((2 * width, tile_order), BF16)],
        ),
        out_shape=jax.ShapeDtypeStruct((columns.steps, 2, half_rows * width, tile_order), BF16),
        compiler_params=PARAMS,
        cost_estimate=cost(12 * half_rows * columns.steps * width * tile_order * tile_order),
        name="left_products",
    )(*tables, *[tiles] * per_step, *q_pieces)


def packed_first(blocks):
    return max(1, blocks * 3 // 4)


def packed_place(slots, first_row, first_col, half_rows, half_cols, block_cols, block):
    before = here = count = jnp.int32(0)
    for index in range(half_rows * half_cols):
        place = (first_row + index % half_rows) * block_cols + first_col + index // half_rows
        flag = (slots[place] >= 0).astype(jnp.int32)
        before = before + jnp.where(index < block, flag, 0)
        here = here + jnp.where(index == block, flag, 0)
        count = count + flag
    return jnp.where(here == 1, before, count + block - before), here == 1


def quarter_live(table, first_row, first_col, half_rows, half_cols, block_cols):
    count = jnp.int32(0)
    for index in range(half_rows * half_cols):
        place = (first_row + index % half_rows) * block_cols + first_col + index // half_rows
        count = count + (table[place] >= 0).astype(jnp.int32)
    return count


def right_kernel(columns, block_cols, half_rows, starts, *refs):
    me, slots, mate_slots, row_partner, col_partner, w_ref = refs[:6]
    pieces = refs[6 : 6 + len(starts)]
    step = pl.program_id(0)
    tile_order = w_ref.shape[3]
    width = pieces[0].shape[1]
    packs = columns.kind == Columns.REST
    outs = refs[6 + len(starts) : -3 if packs else -2]
    p_high, p_low = refs[-2:]

    @pl.when(step == 0)
    def _():
        half = columns.half(step, me, row_partner, col_partner)
        for (start, filled), piece in zip(starts, pieces):
            wanted = start(me) >= 0
            if columns.given:
                wanted = div(start(me), columns.half_cols * tile_order) == half
            if filled is not None:
                wanted &= filled(me)

            @pl.when(wanted)
            def _():
                depth = piece.shape[0]
                rows = pl.ds(pl.multiple_of(start(me), depth), depth)
                p_high[rows, :], p_low[rows, :] = split(piece[...])

    column = columns.column(step, me, row_partner, col_partner)
    rows = pl.ds(pl.multiple_of(column * tile_order, tile_order), tile_order)
    both = w_ref[step if columns.given else 0].reshape(2 * w_ref.shape[2], tile_order)
    block = product(both, p_high[rows, :], p_low[rows, :])
    half_cols = columns.half_cols
    if not packs:
        for index, out in enumerate(outs):

            @pl.when(jnp.minimum(step, half_cols) == index)
            def _():
                out[...] = block

        return
    branch, *outs = outs
    packed = refs[-3]
    first_row = half_of(True, me, row_partner) * half_rows
    first_col = columns.half(step, me, row_partner, col_partner) * half_cols
    for row in range(half_rows):
        place, _ = packed_place(
            slots, first_row, first_col, half_rows, half_cols, block_cols, step * half_rows + row
        )
        packed[place] = block[row * width : (row + 1) * width]

    @pl.when(step == half_cols - 1)
    def _():
        count = outs[0].shape[0]
        outs[0][...] = packed[:count]
        for index, out in enumerate(outs[1:]):
            out[...] = packed[count + index]
        keeps = (me[1] > col_partner[me[0], me[1]]).astype(jnp.int32)
        mate_row = half_of(False, me, row_partner) * half_rows
        quarter = half_rows, half_cols, block_cols
        most = jnp.maximum(
            quarter_live(slots, first_row, first_col, *quarter),
            quarter_live(mate_slots, mate_row, keeps * half_cols, *quarter),
        )
        choice = jnp.clip(most - count, 0, len(outs) - 1)
        branch[0] = ((me[0] ^ row_partner[me[0], me[1]]) - 1) * len(outs) + choice


def right_products(kind, tables, w, shards, half_rows, block_cols):
    _, _, height, tile_order = w.shape
    columns = Columns(kind, block_cols)
    half_cols = columns.half_cols
    width = shards[0][0].shape[1]
    blocks = half_rows * half_cols

    whole = pl.BlockSpec(memory_space=pltpu.VMEM)
    one_column = pl.BlockSpec((1, 2, height, tile_order), lambda i, *_: (i, 0, 0, 0))
    scratch = [pltpu.VMEM((block_cols * tile_order, width), BF16)] * 2
    if kind == Columns.REST:
        most = packed_first(blocks)
        shapes = [(most, width, width)] + [(width, width)] * (blocks - most)
        out_specs = [pl.BlockSpec(memory_space=pltpu.SMEM)]
        out_specs += [pl.BlockSpec(shape, lambda i, *_, n=len(shape): (0,) * n) for shape in shapes]
        scratch = [pltpu.VMEM((blocks, width, width), F32)] + scratch
    else:
        shapes = [(height, width)] * half_cols
        out_specs = [pl.BlockSpec((height, width), lambda i, *_: (0, 0))] * half_cols
        if kind == Columns.KEPT:
            shapes += [(height, half_cols * width)]
            out_specs += [
                pl.BlockSpec((height, width), lambda i, *_: (0, jnp.maximum(i - half_cols, 0)))
            ]
    out_shape = [jax.ShapeDtypeStruct(shape, F32) for shape in shapes]
    if kind == Columns.REST:
        out_shape = [jax.ShapeDtypeStruct((1,), jnp.int32)] + out_shape
    return pl.pallas_call(
        functools.partial(
            right_kernel, columns, block_cols, half_rows, [shard[1:] for shard in shards]
        ),
        grid_spec=pltpu.PrefetchScalarGridSpec(
            num_scalar_prefetch=5,
            grid=(columns.steps,),
            in_specs=[whole if columns.given else one_column] + [whole] * len(shards),
            out_specs=out_specs,
            scratch_shapes=scratch,
        ),
        out_shape=out_shape,
        compiler_params=PARAMS,
        cost_estimate=cost(6 * columns.steps * height * width * tile_order),
        name="right_products",
    )(*tables, w, *[shard[0] for shard in shards])


def comes_from(which, me, col_partner):
    distance = me[1] ^ col_partner[me[0], me[1]]
    core = rem(distance, 2) == 1
    return core if which == 0 else jnp.logical_not(core) & (div(distance, 2) == which - 1)


def sum_kernel(half_rows, block_cols, singles, sections, *refs):
    me, _, mate_slots, row_partner, col_partner, kept_ref, packed_ref = refs[:7]
    single_refs, section_refs, out = refs[7 : 7 + singles], refs[7 + singles : -1], refs[-1]
    half_cols = block_cols // 2
    step = pl.program_id(0)
    keeps = (me[1] > col_partner[me[0], me[1]]).astype(jnp.int32)
    first_row = half_of(False, me, row_partner) * half_rows
    place, live = packed_place(
        mate_slots, first_row, keeps * half_cols, half_rows, half_cols, block_cols, step
    )
    count = packed_ref.shape[0]
    at = 0
    for index, kind in enumerate(sections):
        for which in range(kind):
            section = section_refs[at + which]
            wanted = div(step, half_rows) == index
            if kind > 1:
                wanted &= comes_from(which, me, col_partner)

            @pl.when(wanted)
            def _():
                out[...] = kept_ref[...] + section[...].reshape(out.shape)

        at += kind

    @pl.when(live & (place < count))
    def _():
        out[...] += packed_ref[jnp.minimum(place, count - 1)]

    for index, single in enumerate(single_refs):

        @pl.when(live & (place == count + index))
        def _():
            out[...] += single[...]


def sum_blocks(tables, half_rows, block_cols, kept, packed, singles, sections):
    half_cols = block_cols // 2
    height, both = kept.shape
    width = both // half_cols
    block = pl.BlockSpec((width, width), lambda i, *_: (rem(i, half_rows), div(i, half_rows)))

    def section_spec(index, section, which=None):
        def section_at(i, me, slots, mate_slots, row_partner, col_partner):
            here = jnp.clip(i - index * half_rows, 0, half_rows - 1)
            if which is not None:
                here = jnp.where(comes_from(which, me, col_partner), here, 0)
            if section.ndim == 2:
                return here, 0
            return index if which == 0 else col_partner[me[0], me[1]], here, 0

        return pl.BlockSpec((1,) * (section.ndim - 2) + (width, width), section_at)

    return pl.pallas_call(
        functools.partial(
            sum_kernel, half_rows, block_cols, len(singles), [len(each) for each in sections]
        ),
        grid_spec=pltpu.PrefetchScalarGridSpec(
            num_scalar_prefetch=5,
            grid=(half_rows * half_cols,),
            in_specs=[block]
            + [pl.BlockSpec(memory_space=pltpu.VMEM)] * (1 + len(singles))
            + [
                section_spec(index, each, which if len(group) > 1 else None)
                for index, group in enumerate(sections)
                for which, each in enumerate(group)
            ],
            out_specs=block,
        ),
        out_shape=jax.ShapeDtypeStruct((height, both), F32),
        compiler_params=PARAMS,
        name="sum_blocks",
    )(*tables, kept, packed, *singles, *[each for group in sections for each in group])


def wished_kernel(wish, *refs):
    *sections, wanted = refs
    for index, section in enumerate(sections):

        @pl.when((pl.program_id(0) == index // 4) & (wish[0] == index % 4))
        def _():
            wanted[0] = section[...]


def wished(wish, overs):
    height, width = overs[0][0].shape
    steps = 2 if height % 16 == 0 else 1

    def chip_spec(column, chip):
        def chip_at(b, i, wish):
            here = jnp.where(b == column, i, jnp.where(b < column, 0, steps - 1))
            return jnp.where(wish[0] == chip, here, 0), 0

        return pl.BlockSpec((height // steps, width), chip_at)

    return pl.pallas_call(
        wished_kernel,
        grid_spec=pltpu.PrefetchScalarGridSpec(
            num_scalar_prefetch=1,
            grid=(len(overs), steps),
            in_specs=[chip_spec(b, chip) for b in range(len(overs)) for chip in range(4)],
            out_specs=pl.BlockSpec((1, height // steps, width), lambda b, i, _: (b, i, 0)),
        ),
        out_shape=jax.ShapeDtypeStruct((len(overs), height, width), F32),
        compiler_params=PARAMS,
        cost_estimate=cost(0),
        name="wished",
    )(wish, *[section for over in overs for section in over])


def flip(value, axis, size, mask):
    return lax.ppermute(value, axis, [(i, i ^ mask) for i in range(size)])


def hand_out(part, axis):
    return lax.ppermute(part, axis, [(1, 0), (2, 3)])


def first_prolong(shard, axis, size):
    if size != 4:
        return None
    part = shard.shape[0] // 2
    by_two = [flip(each, axis, size, 2) for each in (shard[:part], shard[part:])]
    near = [*by_two, flip(shard, axis, size, 1), lax.ppermute(shard, axis, [(1, 2), (2, 1)])]
    return near + [hand_out(by_two[0], axis)]


def gather_prolong(shard, near, axis, size):
    depth = shard.shape[0]
    if near is None:
        gathered = lax.all_gather(shard, axis)
        return [(gathered[i], lambda me, i=i: jnp.int32(i * depth), None) for i in range(size)]
    *by_two, by_one, middle, handed = near
    handed = [handed, hand_out(by_two[1], axis)]

    def at(mask, first=0):
        return lambda me: (me[0] ^ mask) * depth + first

    def inner(me):
        return (me[0] == 1) | (me[0] == 2)

    pieces = [(shard, at(0), None), (by_one, at(1), None), (middle, at(3), inner)]
    for index in range(2):
        first = index * (depth // 2)
        pieces.append((by_two[index], at(2, first), None))
        pieces.append((handed[index], at(3, first), lambda me: jnp.logical_not(inner(me))))
    return pieces


def gather_restrict(shard, near, slots, axis, size):
    over_x = flip(shard, axis, size, 2)
    over_y = flip(shard, axis, size, 4)
    if near is not None:
        over_x, near[0], slots = lax.optimization_barrier((over_x, near[0], slots))
    pieces = [shard, over_x, over_y, flip(over_x, axis, size, 4)]
    if near is not None:
        pieces, near[1:3], near[4] = lax.optimization_barrier((pieces, near[1:3], near[4]))
    mine = jnp.stack(pieces)
    return [mine, flip(mine, axis, size, 1)], slots


def pair_switch(index, size, branch, operand, choices=1):
    branches = [
        functools.partial(branch, mask, choice) for mask in range(1, size) for choice in range(choices)
    ]
    return lax.switch(index[0], branches, operand)


def solution(mesh):
    n_row = mesh.shape["row"]
    n_col = mesh.shape["col"]

    def body(tiles, coords, counts, restrict, prolong, row_partner, col_partner):
        tile_order = tiles.shape[1]
        block_rows = restrict.shape[0] * n_col // tile_order
        block_cols = prolong.shape[0] * n_row // tile_order
        half_rows, half_cols = block_rows // 2, block_cols // 2
        row = lax.axis_index("row").astype(jnp.int32)
        col = lax.axis_index("col").astype(jnp.int32)
        me = jnp.stack([row, col])

        row_partner, coords = row_partner.T, coords.T
        places = block_rows * block_cols
        slots, first, wish = make_tables(
            me, row_partner, col_partner, coords, counts, places, block_cols
        )
        near = first_prolong(prolong, "row", n_row)
        by_chip = n_col == 8 and block_rows == 4 and tile_order == 2 * restrict.shape[0]
        if by_chip:
            q_pieces, slots = gather_restrict(restrict, near, slots, "col", n_col)
        else:
            q_pieces = [lax.all_gather(restrict, "col", axis=0, tiled=True)]

        shards = gather_prolong(prolong, near, "row", n_row)

        def products(kind, mate_slots):
            tables = (me, slots, row_partner, col_partner)
            w = left_products(kind, tables, tiles, q_pieces, half_rows, block_cols)
            tables = (me, slots, mate_slots, row_partner, col_partner)
            return right_products(kind, tables, w, shards, half_rows, block_cols)

        def swap_first(mask, _, chunk):
            received = flip(chunk, "row", n_row, mask)
            return received, flip(slots, "row", n_row, mask), products(Columns.KEPT, slots)

        def swap_next(mask, _, operands):
            chunk, mate_slots = operands
            return flip(chunk, "row", n_row, mask), products(Columns.REST, mate_slots)

        def swap_more(mask, _, operands):
            return flip(operands[0], "row", n_row, mask), operands[1:]

        def swap_rest(mask, extra, rest):
            return [
                flip(array, "row", n_row, mask) if index <= extra else array
                for index, array in enumerate(rest)
            ]

        given = products(Columns.ON, slots)
        received, mate_slots, kept = pair_switch(first, n_row, swap_first, given[0])
        sections, rest = [], None
        for index in range(half_cols):
            section = kept[index] + received
            if n_col == 8:
                over = [section] + [flip(section, "col", n_col, 2 * chip) for chip in range(1, 4)]
            else:
                over = [lax.all_gather(section, "col")]
            sections.append(over)
            if index + 1 == half_cols:
                break
            chunk, section = lax.optimization_barrier((given[index + 1], section))
            if index == 0:
                received, rest = pair_switch(first, n_row, swap_next, (chunk, mate_slots))
            else:
                received, *_ = pair_switch(first, n_row, swap_more, (chunk,))
            sections[index], received = lax.optimization_barrier((sections[index], received))
        if rest is None:
            rest = products(Columns.REST, mate_slots)
        second, *rest = rest
        rest, section = lax.optimization_barrier((rest, section))
        rest = pair_switch(second, n_row, swap_rest, rest, len(rest))
        if n_col == 8:
            sections[-1], rest = lax.optimization_barrier((sections[-1], rest))
            handed = flip(wished(wish, sections), "col", n_col, 1)
            sections = [[handed] + over for over in sections]
        packed, *singles = rest
        tables = (me, slots, mate_slots, row_partner, col_partner)
        return sum_blocks(tables, half_rows, block_cols, kept[-1], packed, singles, sections)

    in_specs = (
        P(("row", "col"), None, None),
        P(("row", "col"), None),
        P(("row", "col")),
        P(("row", "col"), None),
        P(("col", "row"), None),
        P(),
        P(),
    )
    return jax.shard_map(
        body, mesh=mesh, in_specs=in_specs, out_specs=P("row", "col"), check_vma=False
    )
```

profile of v0, /device:TPU:3, one launch (start us, length us, event | category | flops | bytes accessed | tf_op | source)
XLA Modules:
  0.0 163.6 jit_solution(15318944296992419138)
XLA Ops:
  1.1 2.4 %collective-permute-start.19 = (f32[256,256]{1,0:T(8,128)S(1)}, f32[256,256]{1,0:T(8,128)S(1)}, u32[]{:S(2)}, u32[]{:S(2)}) collective-permute-start(f32[256,256]{1,0:T(8,128)S(1)} %get-tuple-element.419), channel_id=1, source_target_pairs={{0,16},{8,24},{16,0},{24,8},{1,17},{9,25},{17,1},{25,9},{2,18},{10... | collective-permute-start | bytes 786440 | tf_op jit(solution)/shard_map/ppermute | solution.py:428
  3.7 1.3 collective-permute-start.23
  7.0 1.4 make_tables.1
  8.5 6.4 %collective-permute-done.19.refs_9_ = f32[256,256]{1,0:T(8,128)S(1)} collective-permute-done((f32[256,256]{1,0:T(8,128)S(1)}, f32[256,256]{1,0:T(8,128)S(1)}, u32[]{:S(2)}, u32[]{:S(2)}) %collective-permute-start.19) | collective-permute-done | bytes 262176 | tf_op jit(solution)/shard_map/ppermute | solution.py:428
  14.9 1.2 collective-permute-start.21
  16.1 1.3 collective-permute-start.24
  17.4 7.9 %collective-permute-done.22.refs_11_ = f32[256,256]{1,0:T(8,128)S(1)} collective-permute-done((f32[256,256]{1,0:T(8,128)S(1)}, f32[256,256]{1,0:T(8,128)S(1)}, u32[]{:S(2)}, u32[]{:S(2)}) %collective-permute-start.22) | collective-permute-done | bytes 262176 | tf_op jit(solution)/shard_map/ppermute | solution.py:428
  25.3 6.5 %collective-permute-done.24.refs_10_ = f32[256,256]{1,0:T(8,128)S(1)} collective-permute-done((f32[256,256]{1,0:T(8,128)S(1)}, f32[256,256]{1,0:T(8,128)S(1)}, u32[]{:S(2)}, u32[]{:S(2)}) %collective-permute-start.24) | collective-permute-done | bytes 262176 | tf_op jit(solution)/shard_map/ppermute | solution.py:432
  33.0 2.2 %collective-permute-start.25 = (f32[4,256,256]{2,1,0:T(8,128)S(1)}, f32[4,256,256]{2,1,0:T(8,128)S(1)}, u32[]{:S(2)}, u32[]{:S(2)}) collective-permute-start(f32[4,256,256]{2,1,0:T(8,128)S(1)} %pad_maximum_fusion.refs_6_), channel_id=1, source_target_pairs={{0,1},{1,0},{2,3},{3,2},{4,5},{5,4},{6,7},{7,6},{8,9},{9,8},{10,11... | collective-permute-start | bytes 3145736 | tf_op jit(solution)/shard_map/ppermute | solution.py:428
  35.3 1.5 collective-permute-start.26
  37.4 1.4 collective-permute-start.27
  38.9 5.1 %left_products.13.refs_5_ = bf16[2,2,512,512]{3,2,1,0:T(8,128)(2,1)S(1)} custom-call(s32[2]{0:T(128)S(1)} %pad_add_fusion.me.refs_0_, s32[16]{0:T(128)S(1)} %get-tuple-element.379.refs_1_.refs_2_, s32[4,8]{1,0:T(4,128)} %bitcast.11, s32[4,8]{1,0:T(4,128)} %refs_4_.5, f32[16,512,512]{2,1,0:T(8,128)} %refs_5_.1, f32[16,512,512]{2,1,0:T(8,128)} %refs_5_.1, ...), custom_call_target="tpu_custom_call" | custom-call | flops 3221225472 | tf_op jit(solution)/shard_map/left_products/pallas_call | solution.py:159
  44.0 3.5 %collective-permute-done.27.refs_12_ = f32[256,256]{1,0:T(8,128)} collective-permute-done((f32[256,256]{1,0:T(8,128)S(1)}, f32[256,256]{1,0:T(8,128)}, u32[]{:S(2)}, u32[]{:S(2)}) %collective-permute-start.27) | collective-permute-done | bytes 262176 | tf_op jit(solution)/shard_map/ppermute | solution.py:432
  47.5 4.0 %right_products.13 = (f32[512,256]{1,0:T(8,128)S(1)}, f32[512,256]{1,0:T(8,128)}) custom-call(s32[2]{0:T(128)S(1)} %pad_add_fusion.me.refs_0_, s32[16]{0:T(128)S(1)} %get-tuple-element.379.refs_1_.refs_2_, s32[16]{0:T(128)S(1)} %get-tuple-element.379.refs_1_.refs_2_, s32[4,8]{1,0:T(4,128)S(1)} %bitcast.12, s32[4,8]{1,0:T(4,128)S(1)} %copy-done.19, ...), custom_call_target="tpu_custom_call" | custom-call | flops 805306368 | tf_op jit(solution)/shard_map/right_products/pallas_call | solution.py:293
  51.5 17.3 %conditional.3 = (f32[512,256]{1,0:T(8,128)}, s32[16]{0:T(128)}, f32[512,256]{1,0:T(8,128)S(1)}, f32[512,256]{1,0:T(8,128)}, f32[512,512]{1,0:T(8,128)}) conditional(s32[]{:T(128)} %bitcast.4, (f32[512,256]{1,0:T(8,128)S(1)}, s32[16]{0:T(128)S(1)}, s32[2]{0:T(128)S(1)}, s32[4,8]{1,0:T(4,128)S(1)}, s32[4,8]{1,0:T(4,128)S(1)}, ...), branch_computations={%region_0.0_spmd, %region_1.0_spmd, %region_2.0_spmd} | conditional | flops 8053063680 | bytes 2097528 | solution.py:482
  51.5 2.3 %collective-permute-start.5 = (s32[16]{0:T(128)S(1)}, s32[16]{0:T(128)}, u32[]{:S(2)}, u32[]{:S(2)}) collective-permute-start(s32[16]{0:T(128)S(1)} %get-tuple-element.252.refs_1_.refs_2_), channel_id=1, source_target_pairs={{0,24},{8,16},{16,8},{24,0},{1,25},{9,17},{17,9},{25,1},{2,26},{10... | collective-permute-start | bytes 200 | tf_op jit(solution)/shard_map/cond/branch_2_fun/ppermute | solution.py:428
  54.9 7.4 %left_products.9.refs_5_ = bf16[4,2,512,512]{3,2,1,0:T(8,128)(2,1)S(1)} custom-call(s32[2]{0:T(128)S(1)} %get-tuple-element.253.refs_0_, s32[16]{0:T(128)S(1)} %get-tuple-element.252.refs_1_.refs_2_, s32[4,8]{1,0:T(4,128)S(1)} %get-tuple-element.254.refs_2_.refs_3_, s32[4,8]{1,0:T(4,128)S(1)} %get-tuple-element.255.refs_3_.refs_4_, ...), custom_call_target="tpu_custom_call" | custom-call | flops 6442450944 | tf_op jit(solution)/shard_map/cond/branch_2_fun/left_products/pallas_call | solution.py:159
  62.3 5.7 %right_products.9 = (f32[512,256]{1,0:T(8,128)S(1)}, f32[512,256]{1,0:T(8,128)}, f32[512,512]{1,0:T(8,128)}) custom-call(s32[2]{0:T(128)S(1)} %get-tuple-element.253.refs_0_, s32[16]{0:T(128)S(1)} %get-tuple-element.252.refs_1_.refs_2_, s32[16]{0:T(128)S(1)} %get-tuple-element.252.refs_1_.refs_2_, s32[4,8]{1,0:T(4,128)S(1)} %get-tuple-element.254.refs_2_.refs_3_, ...), custom_call_target="tpu_custom_call" | custom-call | flops 1610612736 | tf_op jit(solution)/shard_map/cond/branch_2_fun/right_products/pallas_call | solution.py:293
  70.2 1.7 %collective-permute-start.29 = (f32[512,256]{1,0:T(8,128)S(1)}, f32[512,256]{1,0:T(8,128)S(1)}, u32[]{:S(2)}, u32[]{:S(2)}) collective-permute-start(f32[512,256]{1,0:T(8,128)S(1)} %add.6.refs_0_.refs_9_), channel_id=1, source_target_pairs={{0,4},{1,5},{2,6},{3,7},{4,0},{5,1},{6,2},{7,3},{8,12},{9,13},{10,... | collective-permute-start | bytes 1572872 | tf_op jit(solution)/shard_map/ppermute | solution.py:428
  72.6 11.0 %conditional.4 = (f32[512,256]{1,0:T(8,128)}, s32[1]{0:T(128)}, f32[3,256,256]{2,1,0:T(8,128)S(1)}, f32[256,256]{1,0:T(8,128)S(1)}) conditional(s32[]{:T(128)} %bitcast.4, (f32[512,256]{1,0:T(8,128)}, s32[2]{0:T(128)S(1)}, s32[16]{0:T(128)S(1)}, s32[4,8]{1,0:T(4,128)S(1)}, s32[4,8]{1,0:T(4,128)S(1)}, ...), branch_computations={%region_3.0_spmd, %region_4.0_spmd, %region_5.0_spmd} | conditional | flops 4026531840 | bytes 8388792 | solution.py:482
  72.6 1.7 %collective-permute-start.8 = (f32[512,256]{1,0:T(8,128)}, f32[512,256]{1,0:T(8,128)}, u32[]{:S(2)}, u32[]{:S(2)}) collective-permute-start(f32[512,256]{1,0:T(8,128)} %get-tuple-element.307), channel_id=1, source_target_pairs={{0,24},{8,16},{16,8},{24,0},{1,25},{9,17},{17,9},{25,1},{2,26},{10... | collective-permute-start | bytes 1572872 | tf_op jit(solution)/shard_map/cond/branch_2_fun/ppermute | solution.py:428
  74.4 5.3 %left_products.12.refs_5_ = bf16[2,2,512,512]{3,2,1,0:T(8,128)(2,1)S(1)} custom-call(s32[2]{0:T(128)S(1)} %get-tuple-element.308.refs_0_, s32[16]{0:T(128)S(1)} %get-tuple-element.309.refs_1_, s32[4,8]{1,0:T(4,128)S(1)} %get-tuple-element.311.refs_2_.refs_3_, s32[4,8]{1,0:T(4,128)S(1)} %get-tuple-element.312.refs_3_.refs_4_, ...), custom_call_target="tpu_custom_call" | custom-call | flops 3221225472 | tf_op jit(solution)/shard_map/cond/branch_2_fun/left_products/pallas_call | solution.py:159
  79.7 3.9 %right_products.12 = (s32[1]{0:T(128)}, f32[3,256,256]{2,1,0:T(8,128)S(1)}, f32[256,256]{1,0:T(8,128)S(1)}) custom-call(s32[2]{0:T(128)S(1)} %get-tuple-element.308.refs_0_, s32[16]{0:T(128)S(1)} %get-tuple-element.309.refs_1_, s32[16]{0:T(128)} %get-tuple-element.310.refs_2_, s32[4,8]{1,0:T(4,128)S(1)} %get-tuple-element.311.refs_2_.refs_3_, ...), custom_call_target="tpu_custom_call" | custom-call | flops 805306368 | tf_op jit(solution)/shard_map/cond/branch_2_fun/right_products/pallas_call | solution.py:293
  84.9 1.3 add.7.refs_4_.refs_14_
  86.2 16.7 %collective-permute-start.31 = (f32[512,256]{1,0:T(8,128)S(1)}, f32[512,256]{1,0:T(8,128)S(1)}, u32[]{:S(2)}, u32[]{:S(2)}) collective-permute-start(f32[512,256]{1,0:T(8,128)S(1)} %add.7.refs_4_.refs_14_), channel_id=1, source_target_pairs={{0,2},{1,3},{2,0},{3,1},{4,6},{5,7},{6,4},{7,5},{8,10},{9,11},{10,... | collective-permute-start | bytes 1572872 | tf_op jit(solution)/shard_map/ppermute | solution.py:428
  102.9 1.3 collective-permute-start.33
  104.8 12.9 %conditional.5 = (f32[3,256,256]{2,1,0:T(8,128)}, f32[256,256]{1,0:T(8,128)S(1)}) conditional(s32[]{:T(128)} %bitcast.9, (f32[3,256,256]{2,1,0:T(8,128)S(1)}, f32[256,256]{1,0:T(8,128)S(1)}) %tuple.66, (f32[3,256,256]{2,1,0:T(8,128)S(1)}, f32[256,256]{1,0:T(8,128)S(1)}) %tuple.66, (f32[3,256,256]{2,1,0:T(8,128)S(1)}, ...), branch_computations={%region_6.0_spmd, %region_7.0_spmd, %region_8.0_spmd, %region_9.0_... | conditional | bytes 4718688 | solution.py:482
  105.0 12.7 %collective-permute-done.15 = f32[3,256,256]{2,1,0:T(8,128)} collective-permute-done((f32[3,256,256]{2,1,0:T(8,128)S(1)}, f32[3,256,256]{2,1,0:T(8,128)}, u32[]{:S(2)}, u32[]{:S(2)}) %collective-permute-start.15) | collective-permute-done | bytes 786464 | tf_op jit(solution)/shard_map/cond/branch_4_fun/ppermute | solution.py:428
  117.8 3.0 %wished.1 = f32[2,512,256]{2,1,0:T(8,128)S(1)} custom-call(s32[1]{0:T(128)} %get-tuple-element.409.wish, f32[512,256]{1,0:T(8,128)S(1)} %add.6.refs_0_.refs_9_, f32[512,256]{1,0:T(8,128)S(1)} %collective-permute-done.28.refs_1_.refs_10_, f32[512,256]{1,0:T(8,128)S(1)} %collective-permute-done.29.refs_2_.refs_11_, ...), custom_call_target="tpu_custom_call" | custom-call | tf_op jit(solution)/shard_map/wished/pallas_call | solution.py:412
  120.9 35.7 %collective-permute-start.34 = (f32[2,512,256]{2,1,0:T(8,128)S(1)}, f32[2,512,256]{2,1,0:T(8,128)S(1)}, u32[]{:S(2)}, u32[]{:S(2)}) collective-permute-start(f32[2,512,256]{2,1,0:T(8,128)S(1)} %wished.1), channel_id=1, source_target_pairs={{0,1},{1,0},{2,3},{3,2},{4,5},{5,4},{6,7},{7,6},{8,9},{9,8},{10,11... | collective-permute-start | bytes 3145736 | tf_op jit(solution)/shard_map/ppermute | solution.py:428
  156.6 2.3 %collective-permute-done.34.refs_8_.refs_13_ = f32[2,512,256]{2,1,0:T(8,128)S(1)} collective-permute-done((f32[2,512,256]{2,1,0:T(8,128)S(1)}, f32[2,512,256]{2,1,0:T(8,128)S(1)}, u32[]{:S(2)}, u32[]{:S(2)}) %collective-permute-start.34) | collective-permute-done | bytes 1048608 | tf_op jit(solution)/shard_map/ppermute | solution.py:428
  158.9 4.7 %sum_blocks.1 = f32[512,512]{1,0:T(8,128)} custom-call(s32[2]{0:T(128)S(1)} %pad_add_fusion.me.refs_0_, s32[16]{0:T(128)S(1)} %get-tuple-element.379.refs_1_.refs_2_, s32[16]{0:T(128)} %get-tuple-element.391.refs_2_, s32[4,8]{1,0:T(4,128)S(1)} %bitcast.19, s32[4,8]{1,0:T(4,128)S(1)} %copy-done.19, f32[512,512]{1,0:T(8,128)S(1)} %copy-done.17, ...), custom_call_target="tpu_custom_call" | custom-call | tf_op jit(solution)/shard_map/sum_blocks/pallas_call | solution.py:370
  (51 shorter events, 9.5 us)
Async XLA Ops:
  1.1 13.8 %collective-permute-start.19 = (f32[256,256]{1,0:T(8,128)S(1)}, f32[256,256]{1,0:T(8,128)S(1)}, u32[]{:S(2)}, u32[]{:S(2)}) collective-permute-start(f32[256,256]{1,0:T(8,128)S(1)} %get-tuple-element.419), channel_id=1, source_target_pairs={{0,16},{8,24},{16,0},{24,8},{1,17},{9,25},{17,1},{25,9},{2,18},{10... | collective-permute-start | bytes 786440 | tf_op jit(solution)/shard_map/ppermute | solution.py:428
  3.4 11.4 %collective-permute-start.18 = (f32[256,256]{1,0:T(8,128)}, f32[256,256]{1,0:T(8,128)S(1)}, u32[]{:S(2)}, u32[]{:S(2)}) collective-permute-start(f32[256,256]{1,0:T(8,128)} %param.22), channel_id=1, source_target_pairs={{0,2},{1,3},{2,0},{3,1},{4,6},{5,7},{6,4},{7,5},{8,10},{9,11},{10,... | collective-permute-start | bytes 786440 | tf_op jit(solution)/shard_map/ppermute | solution.py:428
  3.7 28.1 %collective-permute-start.23 = (f32[512,256]{1,0:T(8,128)}, f32[512,256]{1,0:T(8,128)S(1)}, u32[]{:S(2)}, u32[]{:S(2)}) collective-permute-start(f32[512,256]{1,0:T(8,128)} %refs_6_.1), channel_id=1, source_target_pairs={{0,8},{8,0},{16,24},{24,16},{1,9},{9,1},{17,25},{25,17},{2,10},{10... | collective-permute-start | bytes 1572872 | tf_op jit(solution)/shard_map/ppermute | solution.py:428
  5.0 20.3 %collective-permute-start.20 = (f32[256,256]{1,0:T(8,128)}, f32[256,256]{1,0:T(8,128)S(1)}, u32[]{:S(2)}, u32[]{:S(2)}) collective-permute-start(f32[256,256]{1,0:T(8,128)} %param.22), channel_id=1, source_target_pairs={{0,4},{1,5},{2,6},{3,7},{4,0},{5,1},{6,2},{7,3},{8,12},{9,13},{10,... | collective-permute-start | bytes 786440 | tf_op jit(solution)/shard_map/ppermute | solution.py:428
  6.2 19.1 %collective-permute-start.22 = (f32[256,256]{1,0:T(8,128)S(1)}, f32[256,256]{1,0:T(8,128)S(1)}, u32[]{:S(2)}, u32[]{:S(2)}) collective-permute-start(f32[256,256]{1,0:T(8,128)S(1)} %get-tuple-element.418), channel_id=1, source_target_pairs={{0,16},{8,24},{16,0},{24,8},{1,17},{9,25},{17,1},{25,9},{2,18},{10... | collective-permute-start | bytes 786440 | tf_op jit(solution)/shard_map/ppermute | solution.py:428
  14.9 10.4 %collective-permute-start.21 = (f32[256,256]{1,0:T(8,128)S(1)}, f32[256,256]{1,0:T(8,128)S(1)}, u32[]{:S(2)}, u32[]{:S(2)}) collective-permute-start(f32[256,256]{1,0:T(8,128)S(1)} %collective-permute-done.18), channel_id=1, source_target_pairs={{0,4},{1,5},{2,6},{3,7},{4,0},{5,1},{6,2},{7,3},{8,12},{9,13},{10,... | collective-permute-start | bytes 786440 | tf_op jit(solution)/shard_map/ppermute | solution.py:428
  16.1 15.7 %collective-permute-start.24 = (f32[256,256]{1,0:T(8,128)S(1)}, f32[256,256]{1,0:T(8,128)S(1)}, u32[]{:S(2)}, u32[]{:S(2)}) collective-permute-start(f32[256,256]{1,0:T(8,128)S(1)} %collective-permute-done.19.refs_9_), channel_id=1, source_target_pairs={{8,0},{16,24},{9,1},{17,25},{10,2},{18,26},{11,3},{19,27},{12,4},{... | collective-permute-start | bytes 786440 | tf_op jit(solution)/shard_map/ppermute | solution.py:432
  25.3 26.2 %copy-start.9 = (f32[256,256]{1,0:T(8,128)}, f32[256,256]{1,0:T(8,128)S(1)}, u32[]{:S(2)}) copy-start(f32[256,256]{1,0:T(8,128)S(1)} %collective-permute-done.22.refs_11_) | copy-start | bytes 786436
  31.8 19.7 %copy-start.13 = (f32[256,256]{1,0:T(8,128)}, f32[256,256]{1,0:T(8,128)S(1)}, u32[]{:S(2)}) copy-start(f32[256,256]{1,0:T(8,128)S(1)} %collective-permute-done.24.refs_10_) | copy-start | bytes 786436
  31.8 19.7 %copy-start.5 = (f32[512,256]{1,0:T(8,128)}, f32[512,256]{1,0:T(8,128)S(1)}, u32[]{:S(2)}) copy-start(f32[512,256]{1,0:T(8,128)S(1)} %collective-permute-done.23.refs_7_) | copy-start | bytes 1572868
  33.0 5.8 %collective-permute-start.25 = (f32[4,256,256]{2,1,0:T(8,128)S(1)}, f32[4,256,256]{2,1,0:T(8,128)S(1)}, u32[]{:S(2)}, u32[]{:S(2)}) collective-permute-start(f32[4,256,256]{2,1,0:T(8,128)S(1)} %pad_maximum_fusion.refs_6_), channel_id=1, source_target_pairs={{0,1},{1,0},{2,3},{3,2},{4,5},{5,4},{6,7},{7,6},{8,9},{9,8},{10,11... | collective-permute-start | bytes 3145736 | tf_op jit(solution)/shard_map/ppermute | solution.py:428
  35.3 8.7 %collective-permute-start.26 = (f32[512,256]{1,0:T(8,128)}, f32[512,256]{1,0:T(8,128)}, u32[]{:S(2)}, u32[]{:S(2)}) collective-permute-start(f32[512,256]{1,0:T(8,128)} %refs_6_.1), channel_id=1, source_target_pairs={{8,16},{16,8},{9,17},{17,9},{10,18},{18,10},{11,19},{19,11},{12,20... | collective-permute-start | bytes 1572872 | tf_op jit(solution)/shard_map/ppermute | solution.py:440
  37.4 10.1 %copy-start.1 = (f32[512,256]{1,0:T(8,128)S(1)}, f32[512,256]{1,0:T(8,128)}, u32[]{:S(2)}) copy-start(f32[512,256]{1,0:T(8,128)} %refs_6_.1) | copy-start | bytes 1572868
  37.4 10.1 %copy-start.18 = (s32[8,4]{0,1:T(4,128)S(1)}, s32[8,4]{0,1:T(4,128)}, u32[]{:S(2)}) copy-start(s32[8,4]{0,1:T(4,128)} %param.24) | copy-start | bytes 388
  37.4 10.1 %copy-start.19 = (s32[4,8]{1,0:T(4,128)S(1)}, s32[4,8]{1,0:T(4,128)}, u32[]{:S(2)}) copy-start(s32[4,8]{1,0:T(4,128)} %refs_4_.5) | copy-start | bytes 388
  37.4 10.0 %collective-permute-start.27 = (f32[256,256]{1,0:T(8,128)S(1)}, f32[256,256]{1,0:T(8,128)}, u32[]{:S(2)}, u32[]{:S(2)}) collective-permute-start(f32[256,256]{1,0:T(8,128)S(1)} %collective-permute-done.22.refs_11_), channel_id=1, source_target_pairs={{8,0},{16,24},{9,1},{17,25},{10,2},{18,26},{11,3},{19,27},{12,4},{... | collective-permute-start | bytes 786440 | tf_op jit(solution)/shard_map/ppermute | solution.py:432
  38.9 12.6 %copy-start = (f32[4,256,256]{2,1,0:T(8,128)}, f32[4,256,256]{2,1,0:T(8,128)S(1)}, u32[]{:S(2)}) copy-start(f32[4,256,256]{2,1,0:T(8,128)S(1)} %collective-permute-done.25.refs_7_) | copy-start | bytes 3145732
  51.5 16.4 %collective-permute-start.5 = (s32[16]{0:T(128)S(1)}, s32[16]{0:T(128)}, u32[]{:S(2)}, u32[]{:S(2)}) collective-permute-start(s32[16]{0:T(128)S(1)} %get-tuple-element.252.refs_1_.refs_2_), channel_id=1, source_target_pairs={{0,24},{8,16},{16,8},{24,0},{1,25},{9,17},{17,9},{25,1},{2,26},{10... | collective-permute-start | bytes 200 | tf_op jit(solution)/shard_map/cond/branch_2_fun/ppermute | solution.py:428
  53.9 14.9 %collective-permute-start.4 = (f32[512,256]{1,0:T(8,128)S(1)}, f32[512,256]{1,0:T(8,128)}, u32[]{:S(2)}, u32[]{:S(2)}) collective-permute-start(f32[512,256]{1,0:T(8,128)S(1)} %get-tuple-element.251), channel_id=1, source_target_pairs={{0,24},{8,16},{16,8},{24,0},{1,25},{9,17},{17,9},{25,1},{2,26},{10... | collective-permute-start | bytes 1572872 | tf_op jit(solution)/shard_map/cond/branch_2_fun/ppermute | solution.py:428
  69.9 13.7 %collective-permute-start.28 = (f32[512,256]{1,0:T(8,128)S(1)}, f32[512,256]{1,0:T(8,128)S(1)}, u32[]{:S(2)}, u32[]{:S(2)}) collective-permute-start(f32[512,256]{1,0:T(8,128)S(1)} %add.6.refs_0_.refs_9_), channel_id=1, source_target_pairs={{0,2},{1,3},{2,0},{3,1},{4,6},{5,7},{6,4},{7,5},{8,10},{9,11},{10,... | collective-permute-start | bytes 1572872 | tf_op jit(solution)/shard_map/ppermute | solution.py:428
  70.2 13.5 %collective-permute-start.29 = (f32[512,256]{1,0:T(8,128)S(1)}, f32[512,256]{1,0:T(8,128)S(1)}, u32[]{:S(2)}, u32[]{:S(2)}) collective-permute-start(f32[512,256]{1,0:T(8,128)S(1)} %add.6.refs_0_.refs_9_), channel_id=1, source_target_pairs={{0,4},{1,5},{2,6},{3,7},{4,0},{5,1},{6,2},{7,3},{8,12},{9,13},{10,... | collective-permute-start | bytes 1572872 | tf_op jit(solution)/shard_map/ppermute | solution.py:428
  71.9 13.0 %collective-permute-start.30 = (f32[512,256]{1,0:T(8,128)S(1)}, f32[512,256]{1,0:T(8,128)S(1)}, u32[]{:S(2)}, u32[]{:S(2)}) collective-permute-start(f32[512,256]{1,0:T(8,128)S(1)} %add.6.refs_0_.refs_9_), channel_id=1, source_target_pairs={{0,6},{1,7},{2,4},{3,5},{4,2},{5,3},{6,0},{7,1},{8,14},{9,15},{10,... | collective-permute-start | bytes 1572872 | tf_op jit(solution)/shard_map/ppermute | solution.py:428
  72.6 11.0 %collective-permute-start.8 = (f32[512,256]{1,0:T(8,128)}, f32[512,256]{1,0:T(8,128)}, u32[]{:S(2)}, u32[]{:S(2)}) collective-permute-start(f32[512,256]{1,0:T(8,128)} %get-tuple-element.307), channel_id=1, source_target_pairs={{0,24},{8,16},{16,8},{24,0},{1,25},{9,17},{17,9},{25,1},{2,26},{10... | collective-permute-start | bytes 1572872 | tf_op jit(solution)/shard_map/cond/branch_2_fun/ppermute | solution.py:428
  74.3 5.3 %copy-start.8 = (f32[512,256]{1,0:T(8,128)S(1)}, f32[512,256]{1,0:T(8,128)}, u32[]{:S(2)}) copy-start(f32[512,256]{1,0:T(8,128)} %get-tuple-element.317.refs_7_) | copy-start | bytes 1572868 | tf_op jit(solution)/shard_map/cond
  74.3 5.3 %copy-start.12 = (f32[256,256]{1,0:T(8,128)S(1)}, f32[256,256]{1,0:T(8,128)}, u32[]{:S(2)}) copy-start(f32[256,256]{1,0:T(8,128)} %get-tuple-element.321.refs_11_) | copy-start | bytes 786436 | tf_op jit(solution)/shard_map/cond
  74.3 5.3 %copy-start.16 = (f32[256,256]{1,0:T(8,128)S(1)}, f32[256,256]{1,0:T(8,128)}, u32[]{:S(2)}) copy-start(f32[256,256]{1,0:T(8,128)} %get-tuple-element.320.refs_10_) | copy-start | bytes 786436 | tf_op jit(solution)/shard_map/cond
  86.2 31.5 %collective-permute-start.31 = (f32[512,256]{1,0:T(8,128)S(1)}, f32[512,256]{1,0:T(8,128)S(1)}, u32[]{:S(2)}, u32[]{:S(2)}) collective-permute-start(f32[512,256]{1,0:T(8,128)S(1)} %add.7.refs_4_.refs_14_), channel_id=1, source_target_pairs={{0,2},{1,3},{2,0},{3,1},{4,6},{5,7},{6,4},{7,5},{8,10},{9,11},{10,... | collective-permute-start | bytes 1572872 | tf_op jit(solution)/shard_map/ppermute | solution.py:428
  102.9 14.9 %collective-permute-start.32 = (f32[512,256]{1,0:T(8,128)S(1)}, f32[512,256]{1,0:T(8,128)}, u32[]{:S(2)}, u32[]{:S(2)}) collective-permute-start(f32[512,256]{1,0:T(8,128)S(1)} %add.7.refs_4_.refs_14_), channel_id=1, source_target_pairs={{0,4},{1,5},{2,6},{3,7},{4,0},{5,1},{6,2},{7,3},{8,12},{9,13},{10,... | collective-permute-start | bytes 1572872 | tf_op jit(solution)/shard_map/ppermute | solution.py:428
  102.9 14.9 %collective-permute-start.33 = (f32[512,256]{1,0:T(8,128)S(1)}, f32[512,256]{1,0:T(8,128)}, u32[]{:S(2)}, u32[]{:S(2)}) collective-permute-start(f32[512,256]{1,0:T(8,128)S(1)} %add.7.refs_4_.refs_14_), channel_id=1, source_target_pairs={{0,6},{1,7},{2,4},{3,5},{4,2},{5,3},{6,0},{7,1},{8,14},{9,15},{10,... | collective-permute-start | bytes 1572872 | tf_op jit(solution)/shard_map/ppermute | solution.py:428
  104.9 12.8 %collective-permute-start.15 = (f32[3,256,256]{2,1,0:T(8,128)S(1)}, f32[3,256,256]{2,1,0:T(8,128)}, u32[]{:S(2)}, u32[]{:S(2)}) collective-permute-start(f32[3,256,256]{2,1,0:T(8,128)S(1)} %get-tuple-element.334), channel_id=1, source_target_pairs={{0,24},{8,16},{16,8},{24,0},{1,25},{9,17},{17,9},{25,1},{2,26},{10... | collective-permute-start | bytes 2359304 | tf_op jit(solution)/shard_map/cond/branch_4_fun/ppermute | solution.py:428
  117.7 41.2 %copy-start.17 = (f32[512,512]{1,0:T(8,128)S(1)}, f32[512,512]{1,0:T(8,128)}, u32[]{:S(2)}) copy-start(f32[512,512]{1,0:T(8,128)} %get-tuple-element.392.refs_5_) | copy-start | bytes 3145732
  120.9 38.0 %collective-permute-start.34 = (f32[2,512,256]{2,1,0:T(8,128)S(1)}, f32[2,512,256]{2,1,0:T(8,128)S(1)}, u32[]{:S(2)}, u32[]{:S(2)}) collective-permute-start(f32[2,512,256]{2,1,0:T(8,128)S(1)} %wished.1), channel_id=1, source_target_pairs={{0,1},{1,0},{2,3},{3,2},{4,5},{5,4},{6,7},{7,6},{8,9},{9,8},{10,11... | collective-permute-start | bytes 3145736 | tf_op jit(solution)/shard_map/ppermute | solution.py:428
  (1 other events, 5.3 us)
where the time goes:
time: 164 us
  starting transfers between devices  74.4 us (45%)
  waiting for transfers between devices  41.6 us (25%)
  Pallas kernels  40.5 us (25%)
  other arithmetic  3.65 us (2%)
  between operations  2.14 us (1%)
    ppermute x18, starting transfers between devices, flip(): return lax.ppermute(value, axis, [(i, i ^ mask) for i in range(size)])  70.2 us
    ppermute x18, waiting for transfers between devices, flip(): return lax.ppermute(value, axis, [(i, i ^ mask) for i in range(size)])  31.7 us
    pallas_call x3, Pallas kernels, left_products(): pl.pallas_call(functools.partial(left_kernel, columns, block_cols, half_r...  17.8 us
    pallas_call x3, Pallas kernels, right_products(): pl.pallas_call(functools.partial(right_kernel, columns, block_cols, half_...  13.6 us
    ppermute x2, waiting for transfers between devices, hand_out(): return lax.ppermute(part, axis, [(1, 0), (2, 3)])  9.98 us
    pallas_call x1, Pallas kernels, sum_blocks(): pl.pallas_call(functools.partial(sum_kernel, half_rows, block_cols, len(s...  4.68 us
  transfers between devices with their start and end apart: 21, of which 10 were waited for; matrix products, arithmetic and copies ran while one was open for 0% of the time, Pallas kernels for 18%

commit v1 on v0

--- a/solution.py
+++ b/solution.py
@@ -428,17 +428,11 @@
     return lax.ppermute(value, axis, [(i, i ^ mask) for i in range(size)])
 
 
-def hand_out(part, axis):
-    return lax.ppermute(part, axis, [(1, 0), (2, 3)])
-
-
 def first_prolong(shard, axis, size):
     if size != 4:
         return None
-    part = shard.shape[0] // 2
-    by_two = [flip(each, axis, size, 2) for each in (shard[:part], shard[part:])]
-    near = [*by_two, flip(shard, axis, size, 1), lax.ppermute(shard, axis, [(1, 2), (2, 1)])]
-    return near + [hand_out(by_two[0], axis)]
+    by_two, by_one = flip(shard, axis, size, 2), flip(shard, axis, size, 1)
+    return [by_two, by_one, lax.ppermute(shard, axis, [(1, 2), (2, 1)])]
 
 
 def gather_prolong(shard, near, axis, size):
@@ -446,31 +440,31 @@
     if near is None:
         gathered = lax.all_gather(shard, axis)
         return [(gathered[i], lambda me, i=i: jnp.int32(i * depth), None) for i in range(size)]
-    *by_two, by_one, middle, handed = near
-    handed = [handed, hand_out(by_two[1], axis)]
-
-    def at(mask, first=0):
-        return lambda me: (me[0] ^ mask) * depth + first
+    by_two, by_one, middle = near
+    handed = lax.ppermute(by_two, axis, [(1, 0), (2, 3)])
+
+    def at(mask):
+        return lambda me: (me[0] ^ mask) * depth
 
     def inner(me):
         return (me[0] == 1) | (me[0] == 2)
 
-    pieces = [(shard, at(0), None), (by_one, at(1), None), (middle, at(3), inner)]
-    for index in range(2):
-        first = index * (depth // 2)
-        pieces.append((by_two[index], at(2, first), None))
-        pieces.append((handed[index], at(3, first), lambda me: jnp.logical_not(inner(me))))
-    return pieces
+    return [
+        (shard, at(0), None),
+        (by_one, at(1), None),
+        (by_two, at(2), None),
+        (middle, at(3), inner),
+        (handed, at(3), lambda me: jnp.logical_not(inner(me))),
+    ]
 
 
 def gather_restrict(shard, near, slots, axis, size):
     over_x = flip(shard, axis, size, 2)
     over_y = flip(shard, axis, size, 4)
-    if near is not None:
-        over_x, near[0], slots = lax.optimization_barrier((over_x, near[0], slots))
+    over_x, slots = lax.optimization_barrier((over_x, slots))
     pieces = [shard, over_x, over_y, flip(over_x, axis, size, 4)]
     if near is not None:
-        pieces, near[1:3], near[4] = lax.optimization_barrier((pieces, near[1:3], near[4]))
+        pieces, near[:2] = lax.optimization_barrier((pieces, near[:2]))
     mine = jnp.stack(pieces)
     return [mine, flip(mine, axis, size, 1)], slots
 

time: 164 us -> 162 us (0.988)
  the two profiles are of different devices: /device:TPU:3 before, /device:TPU:7 now
where the time goes in v1:
time: 162 us; the launch traced here: 159 us
  waiting for transfers between devices  95.3 us (59%)
  Pallas kernels  40.8 us (25%)
  starting transfers between devices  16.9 us (10%)
  other arithmetic  3.65 us (2%)
  between operations  2.17 us (1%)
    ppermute x17, waiting for transfers between devices, flip(): return lax.ppermute(value, axis, [(i, i ^ mask) for i in range(size)])  87.1 us
    pallas_call x3, Pallas kernels, left_products(): pl.pallas_call(functools.partial(left_kernel, columns, block_cols, half_r...  18.2 us
    ppermute x17, starting transfers between devices, flip(): return lax.ppermute(value, axis, [(i, i ^ mask) for i in range(size)])  14.2 us
    pallas_call x3, Pallas kernels, right_products(): pl.pallas_call(functools.partial(right_kernel, columns, block_cols, half_...  13.8 us
    ppermute x1, waiting for transfers between devices, gather_prolong(): handed = lax.ppermute(by_two, axis, [(1, 0), (2, 3)])  8.28 us
    pallas_call x1, Pallas kernels, sum_blocks(): pl.pallas_call(functools.partial(sum_kernel, half_rows, block_cols, len(s...  4.45 us
  transfers between devices with their start and end apart: 19, of which 9 were waited for; matrix products, arithmetic and copies ran while one was open for 0% of the time, Pallas kernels for 18%

profile of v1, /device:TPU:7, one launch (start us, length us, event | category | flops | bytes accessed | tf_op | source)
XLA Modules:
  0.0 159.0 jit_solution(17308503948415118095)
XLA Ops:
  0.3 2.3 %collective-permute-start.21 = (f32[512,256]{1,0:T(8,128)}, f32[512,256]{1,0:T(8,128)S(1)}, u32[]{:S(2)}, u32[]{:S(2)}) collective-permute-start(f32[512,256]{1,0:T(8,128)} %refs_6_.1), channel_id=1, source_target_pairs={{0,16},{8,24},{16,0},{24,8},{1,17},{9,25},{17,1},{25,9},{2,18},{10... | collective-permute-start | bytes 1572872 | tf_op jit(solution)/shard_map/ppermute | solution.py:428
  2.6 1.3 collective-permute-start.22
  4.8 1.4 make_tables.1
  6.2 1.2 collective-permute-done.18
  7.6 2.7 %collective-permute-done.19 = f32[256,256]{1,0:T(8,128)S(1)} collective-permute-done((f32[256,256]{1,0:T(8,128)}, f32[256,256]{1,0:T(8,128)S(1)}, u32[]{:S(2)}, u32[]{:S(2)}) %collective-permute-start.19) | collective-permute-done | bytes 262176 | tf_op jit(solution)/shard_map/ppermute | solution.py:428
  10.4 5.6 %collective-permute-done.20 = f32[256,256]{1,0:T(8,128)S(1)} collective-permute-done((f32[256,256]{1,0:T(8,128)S(1)}, f32[256,256]{1,0:T(8,128)S(1)}, u32[]{:S(2)}, u32[]{:S(2)}) %collective-permute-start.20) | collective-permute-done | bytes 262176 | tf_op jit(solution)/shard_map/ppermute | solution.py:428
  16.0 9.4 %collective-permute-done.21.refs_8_ = f32[512,256]{1,0:T(8,128)S(1)} collective-permute-done((f32[512,256]{1,0:T(8,128)}, f32[512,256]{1,0:T(8,128)S(1)}, u32[]{:S(2)}, u32[]{:S(2)}) %collective-permute-start.21) | collective-permute-done | bytes 524320 | tf_op jit(solution)/shard_map/ppermute | solution.py:428
  25.4 1.2 pad_maximum_fusion.refs_6_
  26.6 1.9 %collective-permute-start.23 = (f32[4,256,256]{2,1,0:T(8,128)S(1)}, f32[4,256,256]{2,1,0:T(8,128)S(1)}, u32[]{:S(2)}, u32[]{:S(2)}) collective-permute-start(f32[4,256,256]{2,1,0:T(8,128)S(1)} %pad_maximum_fusion.refs_6_), channel_id=1, source_target_pairs={{0,1},{1,0},{2,3},{3,2},{4,5},{5,4},{6,7},{7,6},{8,9},{9,8},{10,11... | collective-permute-start | bytes 3145736 | tf_op jit(solution)/shard_map/ppermute | solution.py:428
  28.5 1.4 collective-permute-start.24
  30.0 1.3 collective-permute-start.25
  31.9 5.2 %left_products.13.refs_5_ = bf16[2,2,512,512]{3,2,1,0:T(8,128)(2,1)S(1)} custom-call(s32[2]{0:T(128)S(1)} %pad_add_fusion.me.refs_0_, s32[16]{0:T(128)S(1)} %get-tuple-element.341.refs_1_.refs_2_, s32[4,8]{1,0:T(4,128)} %bitcast.11, s32[4,8]{1,0:T(4,128)} %refs_4_.5, f32[16,512,512]{2,1,0:T(8,128)} %refs_5_.1, f32[16,512,512]{2,1,0:T(8,128)} %refs_5_.1, ...), custom_call_target="tpu_custom_call" | custom-call | flops 3221225472 | tf_op jit(solution)/shard_map/left_products/pallas_call | solution.py:159
  37.2 8.3 %collective-permute-done.25.refs_10_ = f32[512,256]{1,0:T(8,128)} collective-permute-done((f32[512,256]{1,0:T(8,128)S(1)}, f32[512,256]{1,0:T(8,128)}, u32[]{:S(2)}, u32[]{:S(2)}) %collective-permute-start.25) | collective-permute-done | bytes 524320 | tf_op jit(solution)/shard_map/ppermute | solution.py:444
  45.5 4.1 %right_products.13 = (f32[512,256]{1,0:T(8,128)S(1)}, f32[512,256]{1,0:T(8,128)}) custom-call(s32[2]{0:T(128)S(1)} %pad_add_fusion.me.refs_0_, s32[16]{0:T(128)S(1)} %get-tuple-element.341.refs_1_.refs_2_, s32[16]{0:T(128)S(1)} %get-tuple-element.341.refs_1_.refs_2_, s32[4,8]{1,0:T(4,128)S(1)} %bitcast.12, s32[4,8]{1,0:T(4,128)S(1)} %copy-done.15, ...), custom_call_target="tpu_custom_call" | custom-call | flops 805306368 | tf_op jit(solution)/shard_map/right_products/pallas_call | solution.py:293
  49.6 26.2 %conditional.3 = (f32[512,256]{1,0:T(8,128)}, s32[16]{0:T(128)}, f32[512,256]{1,0:T(8,128)S(1)}, f32[512,256]{1,0:T(8,128)}, f32[512,512]{1,0:T(8,128)}) conditional(s32[]{:T(128)} %bitcast.4, (f32[512,256]{1,0:T(8,128)S(1)}, s32[16]{0:T(128)S(1)}, s32[2]{0:T(128)S(1)}, s32[4,8]{1,0:T(4,128)S(1)}, s32[4,8]{1,0:T(4,128)S(1)}, ...), branch_computations={%region_0.0_spmd, %region_1.0_spmd, %region_2.0_spmd} | conditional | flops 8053063680 | bytes 2097528 | solution.py:476
  50.6 1.5 collective-permute-start.2
  52.1 7.7 %left_products.8.refs_5_ = bf16[4,2,512,512]{3,2,1,0:T(8,128)(2,1)S(1)} custom-call(s32[2]{0:T(128)S(1)} %get-tuple-element.209.refs_0_, s32[16]{0:T(128)S(1)} %get-tuple-element.208.refs_1_.refs_2_, s32[4,8]{1,0:T(4,128)S(1)} %get-tuple-element.210.refs_2_.refs_3_, s32[4,8]{1,0:T(4,128)S(1)} %get-tuple-element.211.refs_3_.refs_4_, ...), custom_call_target="tpu_custom_call" | custom-call | flops 6442450944 | tf_op jit(solution)/shard_map/cond/branch_1_fun/left_products/pallas_call | solution.py:159
  59.7 5.8 %right_products.8 = (f32[512,256]{1,0:T(8,128)S(1)}, f32[512,256]{1,0:T(8,128)}, f32[512,512]{1,0:T(8,128)}) custom-call(s32[2]{0:T(128)S(1)} %get-tuple-element.209.refs_0_, s32[16]{0:T(128)S(1)} %get-tuple-element.208.refs_1_.refs_2_, s32[16]{0:T(128)S(1)} %get-tuple-element.208.refs_1_.refs_2_, s32[4,8]{1,0:T(4,128)S(1)} %get-tuple-element.210.refs_2_.refs_3_, ...), custom_call_target="tpu_custom_call" | custom-call | flops 1610612736 | tf_op jit(solution)/shard_map/cond/branch_1_fun/right_products/pallas_call | solution.py:293
  65.5 10.3 %collective-permute-done.2 = f32[512,256]{1,0:T(8,128)} collective-permute-done((f32[512,256]{1,0:T(8,128)S(1)}, f32[512,256]{1,0:T(8,128)}, u32[]{:S(2)}, u32[]{:S(2)}) %collective-permute-start.2) | collective-permute-done | bytes 524320 | tf_op jit(solution)/shard_map/cond/branch_1_fun/ppermute | solution.py:428
  75.8 1.1 add.6.refs_0_.refs_9_
  77.1 2.6 %collective-permute-start.28 = (f32[512,256]{1,0:T(8,128)S(1)}, f32[512,256]{1,0:T(8,128)S(1)}, u32[]{:S(2)}, u32[]{:S(2)}) collective-permute-start(f32[512,256]{1,0:T(8,128)S(1)} %add.6.refs_0_.refs_9_), channel_id=1, source_target_pairs={{0,6},{1,7},{2,4},{3,5},{4,2},{5,3},{6,0},{7,1},{8,14},{9,15},{10,... | collective-permute-start | bytes 1572872 | tf_op jit(solution)/shard_map/ppermute | solution.py:428
  79.7 25.9 %conditional.4 = (f32[512,256]{1,0:T(8,128)}, s32[1]{0:T(128)}, f32[3,256,256]{2,1,0:T(8,128)S(1)}, f32[256,256]{1,0:T(8,128)S(1)}) conditional(s32[]{:T(128)} %bitcast.4, (f32[512,256]{1,0:T(8,128)}, s32[2]{0:T(128)S(1)}, s32[16]{0:T(128)S(1)}, s32[4,8]{1,0:T(4,128)S(1)}, s32[4,8]{1,0:T(4,128)S(1)}, ...), branch_computations={%region_3.0_spmd, %region_4.0_spmd, %region_5.0_spmd} | conditional | flops 4026531840 | bytes 8388764 | solution.py:476
  79.7 5.3 %left_products.11.refs_5_ = bf16[2,2,512,512]{3,2,1,0:T(8,128)(2,1)S(1)} custom-call(s32[2]{0:T(128)S(1)} %get-tuple-element.257.refs_0_, s32[16]{0:T(128)S(1)} %get-tuple-element.258.refs_1_, s32[4,8]{1,0:T(4,128)S(1)} %get-tuple-element.260.refs_2_.refs_3_, s32[4,8]{1,0:T(4,128)S(1)} %get-tuple-element.261.refs_3_.refs_4_, ...), custom_call_target="tpu_custom_call" | custom-call | flops 3221225472 | tf_op jit(solution)/shard_map/cond/branch_1_fun/left_products/pallas_call | solution.py:159
  85.0 3.9 %right_products.11 = (s32[1]{0:T(128)}, f32[3,256,256]{2,1,0:T(8,128)S(1)}, f32[256,256]{1,0:T(8,128)S(1)}) custom-call(s32[2]{0:T(128)S(1)} %get-tuple-element.257.refs_0_, s32[16]{0:T(128)S(1)} %get-tuple-element.258.refs_1_, s32[16]{0:T(128)} %get-tuple-element.259.refs_2_, s32[4,8]{1,0:T(4,128)S(1)} %get-tuple-element.260.refs_2_.refs_3_, ...), custom_call_target="tpu_custom_call" | custom-call | flops 805306368 | tf_op jit(solution)/shard_map/cond/branch_1_fun/right_products/pallas_call | solution.py:293
  88.9 16.7 %collective-permute-done.7 = f32[512,256]{1,0:T(8,128)} collective-permute-done((f32[512,256]{1,0:T(8,128)}, f32[512,256]{1,0:T(8,128)}, u32[]{:S(2)}, u32[]{:S(2)}) %collective-permute-start.7) | collective-permute-done | bytes 524320 | tf_op jit(solution)/shard_map/cond/branch_1_fun/ppermute | solution.py:428
  105.6 1.3 add.7.refs_4_.refs_14_
  107.1 2.6 %collective-permute-start.31 = (f32[512,256]{1,0:T(8,128)S(1)}, f32[512,256]{1,0:T(8,128)}, u32[]{:S(2)}, u32[]{:S(2)}) collective-permute-start(f32[512,256]{1,0:T(8,128)S(1)} %add.7.refs_4_.refs_14_), channel_id=1, source_target_pairs={{0,6},{1,7},{2,4},{3,5},{4,2},{5,3},{6,0},{7,1},{8,14},{9,15},{10,... | collective-permute-start | bytes 1572872 | tf_op jit(solution)/shard_map/ppermute | solution.py:428
  110.3 38.6 %conditional.5 = (f32[3,256,256]{2,1,0:T(8,128)}, f32[256,256]{1,0:T(8,128)S(1)}) conditional(s32[]{:T(128)} %bitcast.9, (f32[3,256,256]{2,1,0:T(8,128)S(1)}, f32[256,256]{1,0:T(8,128)S(1)}) %tuple.66, (f32[3,256,256]{2,1,0:T(8,128)S(1)}, f32[256,256]{1,0:T(8,128)S(1)}) %tuple.66, (f32[3,256,256]{2,1,0:T(8,128)S(1)}, ...), branch_computations={%region_6.0_spmd, %region_7.0_spmd, %region_8.0_spmd, %region_9.0_... | conditional | bytes 4718688 | solution.py:476
  110.4 38.4 %collective-permute-done.12 = f32[3,256,256]{2,1,0:T(8,128)} collective-permute-done((f32[3,256,256]{2,1,0:T(8,128)S(1)}, f32[3,256,256]{2,1,0:T(8,128)}, u32[]{:S(2)}, u32[]{:S(2)}) %collective-permute-start.12) | collective-permute-done | bytes 786464 | tf_op jit(solution)/shard_map/cond/branch_2_fun/ppermute | solution.py:428
  148.9 2.9 %wished.1 = f32[2,512,256]{2,1,0:T(8,128)S(1)} custom-call(s32[1]{0:T(128)} %get-tuple-element.369.wish, f32[512,256]{1,0:T(8,128)S(1)} %add.6.refs_0_.refs_9_, f32[512,256]{1,0:T(8,128)S(1)} %collective-permute-done.26.refs_1_.refs_10_, f32[512,256]{1,0:T(8,128)S(1)} %collective-permute-done.27.refs_2_.refs_11_, ...), custom_call_target="tpu_custom_call" | custom-call | tf_op jit(solution)/shard_map/wished/pallas_call | solution.py:412
  151.9 2.6 %collective-permute-done.32.refs_8_.refs_13_ = f32[2,512,256]{2,1,0:T(8,128)S(1)} collective-permute-done((f32[2,512,256]{2,1,0:T(8,128)S(1)}, f32[2,512,256]{2,1,0:T(8,128)S(1)}, u32[]{:S(2)}, u32[]{:S(2)}) %collective-permute-start.32) | collective-permute-done | bytes 1048608 | tf_op jit(solution)/shard_map/ppermute | solution.py:428
  154.5 4.5 %sum_blocks.1 = f32[512,512]{1,0:T(8,128)} custom-call(s32[2]{0:T(128)S(1)} %pad_add_fusion.me.refs_0_, s32[16]{0:T(128)S(1)} %get-tuple-element.341.refs_1_.refs_2_, s32[16]{0:T(128)} %get-tuple-element.351.refs_2_, s32[4,8]{1,0:T(4,128)S(1)} %bitcast.19, s32[4,8]{1,0:T(4,128)S(1)} %copy-done.15, f32[512,512]{1,0:T(8,128)S(1)} %copy-done.13, ...), custom_call_target="tpu_custom_call" | custom-call | tf_op jit(solution)/shard_map/sum_blocks/pallas_call | solution.py:370
  (42 shorter events, 2.2 us)
Async XLA Ops:
  0.0 7.4 %collective-permute-start.18 = (f32[256,256]{1,0:T(8,128)}, f32[256,256]{1,0:T(8,128)S(1)}, u32[]{:S(2)}, u32[]{:S(2)}) collective-permute-start(f32[256,256]{1,0:T(8,128)} %param.22), channel_id=1, source_target_pairs={{0,2},{1,3},{2,0},{3,1},{4,6},{5,7},{6,4},{7,5},{8,10},{9,11},{10,... | collective-permute-start | bytes 786440 | tf_op jit(solution)/shard_map/ppermute | solution.py:428
  0.3 25.2 %collective-permute-start.21 = (f32[512,256]{1,0:T(8,128)}, f32[512,256]{1,0:T(8,128)S(1)}, u32[]{:S(2)}, u32[]{:S(2)}) collective-permute-start(f32[512,256]{1,0:T(8,128)} %refs_6_.1), channel_id=1, source_target_pairs={{0,16},{8,24},{16,0},{24,8},{1,17},{9,25},{17,1},{25,9},{2,18},{10... | collective-permute-start | bytes 1572872 | tf_op jit(solution)/shard_map/ppermute | solution.py:428
  2.6 22.9 %collective-permute-start.22 = (f32[512,256]{1,0:T(8,128)}, f32[512,256]{1,0:T(8,128)S(1)}, u32[]{:S(2)}, u32[]{:S(2)}) collective-permute-start(f32[512,256]{1,0:T(8,128)} %refs_6_.1), channel_id=1, source_target_pairs={{0,8},{8,0},{16,24},{24,16},{1,9},{9,1},{17,25},{25,17},{2,10},{10... | collective-permute-start | bytes 1572872 | tf_op jit(solution)/shard_map/ppermute | solution.py:428
  3.9 6.5 %collective-permute-start.19 = (f32[256,256]{1,0:T(8,128)}, f32[256,256]{1,0:T(8,128)S(1)}, u32[]{:S(2)}, u32[]{:S(2)}) collective-permute-start(f32[256,256]{1,0:T(8,128)} %param.22), channel_id=1, source_target_pairs={{0,4},{1,5},{2,6},{3,7},{4,0},{5,1},{6,2},{7,3},{8,12},{9,13},{10,... | collective-permute-start | bytes 786440 | tf_op jit(solution)/shard_map/ppermute | solution.py:428
  7.4 8.6 %collective-permute-start.20 = (f32[256,256]{1,0:T(8,128)S(1)}, f32[256,256]{1,0:T(8,128)S(1)}, u32[]{:S(2)}, u32[]{:S(2)}) collective-permute-start(f32[256,256]{1,0:T(8,128)S(1)} %collective-permute-done.18), channel_id=1, source_target_pairs={{0,4},{1,5},{2,6},{3,7},{4,0},{5,1},{6,2},{7,3},{8,12},{9,13},{10,... | collective-permute-start | bytes 786440 | tf_op jit(solution)/shard_map/ppermute | solution.py:428
  25.4 24.2 %copy-start.5 = (f32[512,256]{1,0:T(8,128)}, f32[512,256]{1,0:T(8,128)S(1)}, u32[]{:S(2)}) copy-start(f32[512,256]{1,0:T(8,128)S(1)} %collective-permute-done.21.refs_8_) | copy-start | bytes 1572868
  25.4 24.2 %copy-start.9 = (f32[512,256]{1,0:T(8,128)}, f32[512,256]{1,0:T(8,128)S(1)}, u32[]{:S(2)}) copy-start(f32[512,256]{1,0:T(8,128)S(1)} %collective-permute-done.22.refs_7_) | copy-start | bytes 1572868
  26.6 5.3 %collective-permute-start.23 = (f32[4,256,256]{2,1,0:T(8,128)S(1)}, f32[4,256,256]{2,1,0:T(8,128)S(1)}, u32[]{:S(2)}, u32[]{:S(2)}) collective-permute-start(f32[4,256,256]{2,1,0:T(8,128)S(1)} %pad_maximum_fusion.refs_6_), channel_id=1, source_target_pairs={{0,1},{1,0},{2,3},{3,2},{4,5},{5,4},{6,7},{7,6},{8,9},{9,8},{10,11... | collective-permute-start | bytes 3145736 | tf_op jit(solution)/shard_map/ppermute | solution.py:428
  28.5 8.7 %collective-permute-start.24 = (f32[512,256]{1,0:T(8,128)}, f32[512,256]{1,0:T(8,128)}, u32[]{:S(2)}, u32[]{:S(2)}) collective-permute-start(f32[512,256]{1,0:T(8,128)} %refs_6_.1), channel_id=1, source_target_pairs={{8,16},{16,8},{9,17},{17,9},{10,18},{18,10},{11,19},{19,11},{12,20... | collective-permute-start | bytes 1572872 | tf_op jit(solution)/shard_map/ppermute | solution.py:435
  30.0 15.5 %collective-permute-start.25 = (f32[512,256]{1,0:T(8,128)S(1)}, f32[512,256]{1,0:T(8,128)}, u32[]{:S(2)}, u32[]{:S(2)}) collective-permute-start(f32[512,256]{1,0:T(8,128)S(1)} %collective-permute-done.21.refs_8_), channel_id=1, source_target_pairs={{8,0},{16,24},{9,1},{17,25},{10,2},{18,26},{11,3},{19,27},{12,4},{... | collective-permute-start | bytes 1572872 | tf_op jit(solution)/shard_map/ppermute | solution.py:444
  31.9 13.6 %copy-start.1 = (f32[512,256]{1,0:T(8,128)S(1)}, f32[512,256]{1,0:T(8,128)}, u32[]{:S(2)}) copy-start(f32[512,256]{1,0:T(8,128)} %refs_6_.1) | copy-start | bytes 1572868
  31.9 13.6 %copy-start.14 = (s32[8,4]{0,1:T(4,128)S(1)}, s32[8,4]{0,1:T(4,128)}, u32[]{:S(2)}) copy-start(s32[8,4]{0,1:T(4,128)} %param.24) | copy-start | bytes 388
  31.9 13.6 %copy-start.15 = (s32[4,8]{1,0:T(4,128)S(1)}, s32[4,8]{1,0:T(4,128)}, u32[]{:S(2)}) copy-start(s32[4,8]{1,0:T(4,128)} %refs_4_.5) | copy-start | bytes 388
  31.9 17.7 %copy-start = (f32[4,256,256]{2,1,0:T(8,128)}, f32[4,256,256]{2,1,0:T(8,128)S(1)}, u32[]{:S(2)}) copy-start(f32[4,256,256]{2,1,0:T(8,128)S(1)} %collective-permute-done.23.refs_7_) | copy-start | bytes 3145732
  49.6 15.9 %collective-permute-start.3 = (s32[16]{0:T(128)S(1)}, s32[16]{0:T(128)}, u32[]{:S(2)}, u32[]{:S(2)}) collective-permute-start(s32[16]{0:T(128)S(1)} %get-tuple-element.208.refs_1_.refs_2_), channel_id=1, source_target_pairs={{0,16},{8,24},{16,0},{24,8},{1,17},{9,25},{17,1},{25,9},{2,18},{10... | collective-permute-start | bytes 200 | tf_op jit(solution)/shard_map/cond/branch_1_fun/ppermute | solution.py:428
  50.6 25.3 %collective-permute-start.2 = (f32[512,256]{1,0:T(8,128)S(1)}, f32[512,256]{1,0:T(8,128)}, u32[]{:S(2)}, u32[]{:S(2)}) collective-permute-start(f32[512,256]{1,0:T(8,128)S(1)} %get-tuple-element.207), channel_id=1, source_target_pairs={{0,16},{8,24},{16,0},{24,8},{1,17},{9,25},{17,1},{25,9},{2,18},{10... | collective-permute-start | bytes 1572872 | tf_op jit(solution)/shard_map/cond/branch_1_fun/ppermute | solution.py:428
  77.0 28.7 %collective-permute-start.26 = (f32[512,256]{1,0:T(8,128)S(1)}, f32[512,256]{1,0:T(8,128)S(1)}, u32[]{:S(2)}, u32[]{:S(2)}) collective-permute-start(f32[512,256]{1,0:T(8,128)S(1)} %add.6.refs_0_.refs_9_), channel_id=1, source_target_pairs={{0,2},{1,3},{2,0},{3,1},{4,6},{5,7},{6,4},{7,5},{8,10},{9,11},{10,... | collective-permute-start | bytes 1572872 | tf_op jit(solution)/shard_map/ppermute | solution.py:428
  77.0 28.6 %collective-permute-start.27 = (f32[512,256]{1,0:T(8,128)S(1)}, f32[512,256]{1,0:T(8,128)S(1)}, u32[]{:S(2)}, u32[]{:S(2)}) collective-permute-start(f32[512,256]{1,0:T(8,128)S(1)} %add.6.refs_0_.refs_9_), channel_id=1, source_target_pairs={{0,4},{1,5},{2,6},{3,7},{4,0},{5,1},{6,2},{7,3},{8,12},{9,13},{10,... | collective-permute-start | bytes 1572872 | tf_op jit(solution)/shard_map/ppermute | solution.py:428
  77.1 28.5 %collective-permute-start.28 = (f32[512,256]{1,0:T(8,128)S(1)}, f32[512,256]{1,0:T(8,128)S(1)}, u32[]{:S(2)}, u32[]{:S(2)}) collective-permute-start(f32[512,256]{1,0:T(8,128)S(1)} %add.6.refs_0_.refs_9_), channel_id=1, source_target_pairs={{0,6},{1,7},{2,4},{3,5},{4,2},{5,3},{6,0},{7,1},{8,14},{9,15},{10,... | collective-permute-start | bytes 1572872 | tf_op jit(solution)/shard_map/ppermute | solution.py:428
  79.7 25.9 %collective-permute-start.7 = (f32[512,256]{1,0:T(8,128)}, f32[512,256]{1,0:T(8,128)}, u32[]{:S(2)}, u32[]{:S(2)}) collective-permute-start(f32[512,256]{1,0:T(8,128)} %get-tuple-element.256), channel_id=1, source_target_pairs={{0,16},{8,24},{16,0},{24,8},{1,17},{9,25},{17,1},{25,9},{2,18},{10... | collective-permute-start | bytes 1572872 | tf_op jit(solution)/shard_map/cond/branch_1_fun/ppermute | solution.py:428
  79.7 5.3 %copy-start.3 = (f32[512,256]{1,0:T(8,128)S(1)}, f32[512,256]{1,0:T(8,128)}, u32[]{:S(2)}) copy-start(f32[512,256]{1,0:T(8,128)} %get-tuple-element.265.refs_6_) | copy-start | bytes 1572868 | tf_op jit(solution)/shard_map/cond
  79.7 5.3 %copy-start.7 = (f32[512,256]{1,0:T(8,128)S(1)}, f32[512,256]{1,0:T(8,128)}, u32[]{:S(2)}) copy-start(f32[512,256]{1,0:T(8,128)} %get-tuple-element.267.refs_8_) | copy-start | bytes 1572868 | tf_op jit(solution)/shard_map/cond
  79.7 5.3 %copy-start.11 = (f32[512,256]{1,0:T(8,128)S(1)}, f32[512,256]{1,0:T(8,128)}, u32[]{:S(2)}) copy-start(f32[512,256]{1,0:T(8,128)} %get-tuple-element.266.refs_7_) | copy-start | bytes 1572868 | tf_op jit(solution)/shard_map/cond
  106.9 42.0 %collective-permute-start.29 = (f32[512,256]{1,0:T(8,128)S(1)}, f32[512,256]{1,0:T(8,128)S(1)}, u32[]{:S(2)}, u32[]{:S(2)}) collective-permute-start(f32[512,256]{1,0:T(8,128)S(1)} %add.7.refs_4_.refs_14_), channel_id=1, source_target_pairs={{0,2},{1,3},{2,0},{3,1},{4,6},{5,7},{6,4},{7,5},{8,10},{9,11},{10,... | collective-permute-start | bytes 1572872 | tf_op jit(solution)/shard_map/ppermute | solution.py:428
  107.0 41.9 %collective-permute-start.30 = (f32[512,256]{1,0:T(8,128)S(1)}, f32[512,256]{1,0:T(8,128)}, u32[]{:S(2)}, u32[]{:S(2)}) collective-permute-start(f32[512,256]{1,0:T(8,128)S(1)} %add.7.refs_4_.refs_14_), channel_id=1, source_target_pairs={{0,4},{1,5},{2,6},{3,7},{4,0},{5,1},{6,2},{7,3},{8,12},{9,13},{10,... | collective-permute-start | bytes 1572872 | tf_op jit(solution)/shard_map/ppermute | solution.py:428
  107.1 41.8 %collective-permute-start.31 = (f32[512,256]{1,0:T(8,128)S(1)}, f32[512,256]{1,0:T(8,128)}, u32[]{:S(2)}, u32[]{:S(2)}) collective-permute-start(f32[512,256]{1,0:T(8,128)S(1)} %add.7.refs_4_.refs_14_), channel_id=1, source_target_pairs={{0,6},{1,7},{2,4},{3,5},{4,2},{5,3},{6,0},{7,1},{8,14},{9,15},{10,... | collective-permute-start | bytes 1572872 | tf_op jit(solution)/shard_map/ppermute | solution.py:428
  110.3 38.5 %collective-permute-start.12 = (f32[3,256,256]{2,1,0:T(8,128)S(1)}, f32[3,256,256]{2,1,0:T(8,128)}, u32[]{:S(2)}, u32[]{:S(2)}) collective-permute-start(f32[3,256,256]{2,1,0:T(8,128)S(1)} %get-tuple-element.294), channel_id=1, source_target_pairs={{0,16},{8,24},{16,0},{24,8},{1,17},{9,25},{17,1},{25,9},{2,18},{10... | collective-permute-start | bytes 2359304 | tf_op jit(solution)/shard_map/cond/branch_2_fun/ppermute | solution.py:428
  148.9 5.7 %copy-start.13 = (f32[512,512]{1,0:T(8,128)S(1)}, f32[512,512]{1,0:T(8,128)}, u32[]{:S(2)}) copy-start(f32[512,512]{1,0:T(8,128)} %get-tuple-element.352.refs_5_) | copy-start | bytes 3145732
  151.8 2.7 %collective-permute-start.32 = (f32[2,512,256]{2,1,0:T(8,128)S(1)}, f32[2,512,256]{2,1,0:T(8,128)S(1)}, u32[]{:S(2)}, u32[]{:S(2)}) collective-permute-start(f32[2,512,256]{2,1,0:T(8,128)S(1)} %wished.1), channel_id=1, source_target_pairs={{0,1},{1,0},{2,3},{3,2},{4,5},{5,4},{6,7},{7,6},{8,9},{9,8},{10,11... | collective-permute-start | bytes 3145736 | tf_op jit(solution)/shard_map/ppermute | solution.py:428

commit v2 on v1

--- a/solution.py
+++ b/solution.py
@@ -74,24 +74,22 @@
 
 
 class Columns:
-    ON, REST, KEPT = range(3)
+    FIRST, NEXT, REST, KEPT_ON, KEPT_REST = range(5)
 
     def __init__(self, kind, block_cols):
         self.kind = kind
-        self.given = kind != self.KEPT
+        self.given = kind in (self.FIRST, self.NEXT, self.REST)
         self.half_cols = block_cols // 2
-        self.steps = block_cols if kind == self.KEPT else self.half_cols
-
-    def half(self, step, me, row_partner, col_partner):
-        if self.kind == self.KEPT:
-            goes_on = (me[1] < col_partner[me[0], me[1]]).astype(jnp.int32)
-            return goes_on ^ div(step, self.half_cols)
-        goes_on = (me[1] < col_partner[row_partner[me[0], me[1]], me[1]]).astype(jnp.int32)
-        return goes_on ^ (1 if self.kind == self.REST else 0)
+        self.skip = 1 if kind == self.NEXT else 0
+        self.steps = 1 if kind == self.FIRST else self.half_cols - self.skip
+
+    def half(self, me, row_partner, col_partner):
+        holder = row_partner[me[0], me[1]] if self.given else me[0]
+        goes_on = (me[1] < col_partner[holder, me[1]]).astype(jnp.int32)
+        return goes_on ^ (1 if self.kind in (self.REST, self.KEPT_REST) else 0)
 
     def column(self, step, me, row_partner, col_partner):
-        half = self.half(step, me, row_partner, col_partner)
-        return half * self.half_cols + rem(step, self.half_cols)
+        return self.half(me, row_partner, col_partner) * self.half_cols + self.skip + step
 
 
 def left_kernel(columns, block_cols, half_rows, per_step, *refs):
@@ -209,29 +207,28 @@
 
     @pl.when(step == 0)
     def _():
-        half = columns.half(step, me, row_partner, col_partner)
+        low = columns.column(0, me, row_partner, col_partner) * tile_order
         for (start, filled), piece in zip(starts, pieces):
-            wanted = start(me) >= 0
-            if columns.given:
-                wanted = div(start(me), columns.half_cols * tile_order) == half
+            begin = start(me)
+            wanted = (begin < low + columns.steps * tile_order) & (begin + piece.shape[0] > low)
             if filled is not None:
                 wanted &= filled(me)
 
             @pl.when(wanted)
             def _():
                 depth = piece.shape[0]
-                rows = pl.ds(pl.multiple_of(start(me), depth), depth)
+                rows = pl.ds(pl.multiple_of(begin, depth), depth)
                 p_high[rows, :], p_low[rows, :] = split(piece[...])
 
     column = columns.column(step, me, row_partner, col_partner)
     rows = pl.ds(pl.multiple_of(column * tile_order, tile_order), tile_order)
-    both = w_ref[step if columns.given else 0].reshape(2 * w_ref.shape[2], tile_order)
+    both = w_ref[step].reshape(2 * w_ref.shape[2], tile_order)
     block = product(both, p_high[rows, :], p_low[rows, :])
     half_cols = columns.half_cols
     if not packs:
         for index, out in enumerate(outs):
 
-            @pl.when(jnp.minimum(step, half_cols) == index)
+            @pl.when((step == index) | (len(outs) == 1))
             def _():
                 out[...] = block
 
@@ -239,7 +236,7 @@
     branch, *outs = outs
     packed = refs[-3]
     first_row = half_of(True, me, row_partner) * half_rows
-    first_col = columns.half(step, me, row_partner, col_partner) * half_cols
+    first_col = columns.half(me, row_partner, col_partner) * half_cols
     for row in range(half_rows):
         place, _ = packed_place(
             slots, first_row, first_col, half_rows, half_cols, block_cols, step * half_rows + row
@@ -271,7 +268,6 @@
     blocks = half_rows * half_cols
 
     whole = pl.BlockSpec(memory_space=pltpu.VMEM)
-    one_column = pl.BlockSpec((1, 2, height, tile_order), lambda i, *_: (i, 0, 0, 0))
     scratch = [pltpu.VMEM((block_cols * tile_order, width), BF16)] * 2
     if kind == Columns.REST:
         most = packed_first(blocks)
@@ -279,14 +275,12 @@
         out_specs = [pl.BlockSpec(memory_space=pltpu.SMEM)]
         out_specs += [pl.BlockSpec(shape, lambda i, *_, n=len(shape): (0,) * n) for shape in shapes]
         scratch = [pltpu.VMEM((blocks, width, width), F32)] + scratch
+    elif kind == Columns.KEPT_REST:
+        shapes = [(height, columns.steps * width)]
+        out_specs = [pl.BlockSpec((height, width), lambda i, *_: (0, i))]
     else:
-        shapes = [(height, width)] * half_cols
-        out_specs = [pl.BlockSpec((height, width), lambda i, *_: (0, 0))] * half_cols
-        if kind == Columns.KEPT:
-            shapes += [(height, half_cols * width)]
-            out_specs += [
-                pl.BlockSpec((height, width), lambda i, *_: (0, jnp.maximum(i - half_cols, 0)))
-            ]
+        shapes = [(height, width)] * columns.steps
+        out_specs = [pl.BlockSpec((height, width), lambda i, *_: (0, 0))] * columns.steps
     out_shape = [jax.ShapeDtypeStruct(shape, F32) for shape in shapes]
     if kind == Columns.REST:
         out_shape = [jax.ShapeDtypeStruct((1,), jnp.int32)] + out_shape
@@ -297,7 +291,7 @@
         grid_spec=pltpu.PrefetchScalarGridSpec(
             num_scalar_prefetch=5,
             grid=(columns.steps,),
-            in_specs=[whole if columns.given else one_column] + [whole] * len(shards),
+            in_specs=[whole] * (1 + len(shards)),
             out_specs=out_specs,
             scratch_shapes=scratch,
         ),
@@ -510,8 +504,8 @@
             return right_products(kind, tables, w, shards, half_rows, block_cols)
 
         def swap_first(mask, _, chunk):
-            received = flip(chunk, "row", n_row, mask)
-            return received, flip(slots, "row", n_row, mask), products(Columns.KEPT, slots)
+            received = flip(chunk, "row", n_row, mask), flip(slots, "row", n_row, mask)
+            return *received, products(Columns.NEXT, slots), products(Columns.KEPT_ON, slots)
 
         def swap_next(mask, _, operands):
             chunk, mate_slots = operands
@@ -521,13 +515,15 @@
             return flip(operands[0], "row", n_row, mask), operands[1:]
 
         def swap_rest(mask, extra, rest):
-            return [
+            received = [
                 flip(array, "row", n_row, mask) if index <= extra else array
                 for index, array in enumerate(rest)
             ]
-
-        given = products(Columns.ON, slots)
-        received, mate_slots, kept = pair_switch(first, n_row, swap_first, given[0])
+            return received, products(Columns.KEPT_REST, slots)
+
+        given = products(Columns.FIRST, slots)
+        received, mate_slots, others, kept = pair_switch(first, n_row, swap_first, given[0])
+        given = [*given, *others]
         sections, rest = [], None
         for index in range(half_cols):
             section = kept[index] + received
@@ -548,14 +544,14 @@
             rest = products(Columns.REST, mate_slots)
         second, *rest = rest
         rest, section = lax.optimization_barrier((rest, section))
-        rest = pair_switch(second, n_row, swap_rest, rest, len(rest))
+        rest, (stays,) = pair_switch(second, n_row, swap_rest, rest, len(rest))
         if n_col == 8:
             sections[-1], rest = lax.optimization_barrier((sections[-1], rest))
             handed = flip(wished(wish, sections), "col", n_col, 1)
             sections = [[handed] + over for over in sections]
         packed, *singles = rest
         tables = (me, slots, mate_slots, row_partner, col_partner)
-        return sum_blocks(tables, half_rows, block_cols, kept[-1], packed, singles, sections)
+        return sum_blocks(tables, half_rows, block_cols, stays, packed, singles, sections)
 
     in_specs = (
         P(("row", "col"), None, None),

time: 162 us -> 159 us (0.981)
  the two profiles are of different devices: /device:TPU:7 before, /device:TPU:3 now
where the time goes in v2:
time: 159 us; the launch traced here: 157 us
  waiting for transfers between devices  78.3 us (49%)
  Pallas kernels  43.6 us (27%)
  starting transfers between devices  20.5 us (13%)
  loops' own time  8.37 us (5%)
  other arithmetic  3.65 us (2%)
  between operations  2.47 us (2%)
    ppermute x17, waiting for transfers between devices, flip(): return lax.ppermute(value, axis, [(i, i ^ mask) for i in range(size)])  68.5 us
    pallas_call x5, Pallas kernels, left_products(): pl.pallas_call(functools.partial(left_kernel, columns, block_cols, half_r...  23.6 us
    ppermute x17, starting transfers between devices, flip(): return lax.ppermute(value, axis, [(i, i ^ mask) for i in range(size)])  18.5 us
    pallas_call x5, Pallas kernels, right_products(): pl.pallas_call(functools.partial(right_kernel, columns, block_cols, half_...  10.9 us
    ppermute x1, waiting for transfers between devices, gather_prolong(): handed = lax.ppermute(by_two, axis, [(1, 0), (2, 3)])  9.72 us
    another operation x3, loops' own time, pair_switch(): return lax.switch(index[0], branches, operand)  8.37 us
    pallas_call x1, Pallas kernels, sum_blocks(): pl.pallas_call(functools.partial(sum_kernel, half_rows, block_cols, len(s...  4.75 us
  transfers between devices with their start and end apart: 19, of which 9 were waited for; matrix products, arithmetic and copies ran while one was open for 0% of the time, Pallas kernels for 22%

profile of v2, /device:TPU:3, one launch (start us, length us, event | category | flops | bytes accessed | tf_op | source)
XLA Modules:
  0.0 156.9 jit_solution(8763799917920802788)
XLA Ops:
  0.1 1.5 collective-permute-start.22
  1.6 2.3 %collective-permute-start.21 = (f32[512,256]{1,0:T(8,128)}, f32[512,256]{1,0:T(8,128)S(1)}, u32[]{:S(2)}, u32[]{:S(2)}) collective-permute-start(f32[512,256]{1,0:T(8,128)} %refs_6_.1), channel_id=1, source_target_pairs={{0,16},{8,24},{16,0},{24,8},{1,17},{9,25},{17,1},{25,9},{2,18},{10... | collective-permute-start | bytes 1572872 | tf_op jit(solution)/shard_map/ppermute | solution.py:422
  5.9 1.4 make_tables.1
  8.7 1.7 %collective-permute-done.19 = f32[256,256]{1,0:T(8,128)S(1)} collective-permute-done((f32[256,256]{1,0:T(8,128)}, f32[256,256]{1,0:T(8,128)S(1)}, u32[]{:S(2)}, u32[]{:S(2)}) %collective-permute-start.19) | collective-permute-done | bytes 262176 | tf_op jit(solution)/shard_map/ppermute | solution.py:422
  10.4 5.6 %collective-permute-done.20 = f32[256,256]{1,0:T(8,128)S(1)} collective-permute-done((f32[256,256]{1,0:T(8,128)S(1)}, f32[256,256]{1,0:T(8,128)S(1)}, u32[]{:S(2)}, u32[]{:S(2)}) %collective-permute-start.20) | collective-permute-done | bytes 262176 | tf_op jit(solution)/shard_map/ppermute | solution.py:422
  16.0 8.2 %collective-permute-done.22.refs_7_ = f32[512,256]{1,0:T(8,128)S(1)} collective-permute-done((f32[512,256]{1,0:T(8,128)}, f32[512,256]{1,0:T(8,128)S(1)}, u32[]{:S(2)}, u32[]{:S(2)}) %collective-permute-start.22) | collective-permute-done | bytes 524320 | tf_op jit(solution)/shard_map/ppermute | solution.py:422
  25.5 4.2 %collective-permute-start.23 = (f32[4,256,256]{2,1,0:T(8,128)S(1)}, f32[4,256,256]{2,1,0:T(8,128)S(1)}, u32[]{:S(2)}, u32[]{:S(2)}) collective-permute-start(f32[4,256,256]{2,1,0:T(8,128)S(1)} %pad_maximum_fusion.refs_5_), channel_id=1, source_target_pairs={{0,1},{1,0},{2,3},{3,2},{4,5},{5,4},{6,7},{7,6},{8,9},{9,8},{10,11... | collective-permute-start | bytes 3145736 | tf_op jit(solution)/shard_map/ppermute | solution.py:422
  30.3 1.3 collective-permute-start.25
  32.3 3.7 %left_products.31.refs_5_ = bf16[1,2,512,512]{3,2,1,0:T(8,128)(2,1)S(1)} custom-call(s32[2]{0:T(128)S(1)} %pad_add_fusion.me.refs_0_, s32[16]{0:T(128)S(1)} %get-tuple-element.553.refs_1_.refs_2_, s32[4,8]{1,0:T(4,128)S(1)} %bitcast.11, s32[4,8]{1,0:T(4,128)S(1)} %copy-done.53, f32[16,512,512]{2,1,0:T(8,128)} %refs_4_.3, ...), custom_call_target="tpu_custom_call" | custom-call | flops 1610612736 | tf_op jit(solution)/shard_map/left_products/pallas_call | solution.py:157
  36.0 9.7 %collective-permute-done.25.refs_10_ = f32[512,256]{1,0:T(8,128)S(1)} collective-permute-done((f32[512,256]{1,0:T(8,128)S(1)}, f32[512,256]{1,0:T(8,128)S(1)}, u32[]{:S(2)}, u32[]{:S(2)}) %collective-permute-start.25) | collective-permute-done | bytes 524320 | tf_op jit(solution)/shard_map/ppermute | solution.py:438
  45.8 1.4 right_products.31
  47.2 32.7 %conditional.3 = (f32[512,256]{1,0:T(8,128)}, s32[16]{0:T(128)}, f32[512,256]{1,0:T(8,128)S(1)}, f32[512,256]{1,0:T(8,128)S(1)}, f32[512,256]{1,0:T(8,128)}) conditional(s32[]{:T(128)} %bitcast.4, (f32[512,256]{1,0:T(8,128)S(1)}, s32[16]{0:T(128)S(1)}, s32[2]{0:T(128)S(1)}, s32[4,8]{1,0:T(4,128)S(1)}, s32[4,8]{1,0:T(4,128)S(1)}, ...), branch_computations={%region_0.0_spmd, %region_1.0_spmd, %region_2.0_spmd} | conditional | flops 6039797760 | bytes 2097528 | solution.py:470
  47.5 2.1 %collective-permute-start.2 = (f32[512,256]{1,0:T(8,128)S(1)}, f32[512,256]{1,0:T(8,128)}, u32[]{:S(2)}, u32[]{:S(2)}) collective-permute-start(f32[512,256]{1,0:T(8,128)S(1)} %get-tuple-element.350), channel_id=1, source_target_pairs={{0,16},{8,24},{16,0},{24,8},{1,17},{9,25},{17,1},{25,9},{2,18},{10... | collective-permute-start | bytes 1572872 | tf_op jit(solution)/shard_map/cond/branch_1_fun/ppermute | solution.py:422
  49.6 4.9 %left_products.19.refs_5_ = bf16[2,2,512,512]{3,2,1,0:T(8,128)(2,1)S(1)} custom-call(s32[2]{0:T(128)S(1)} %get-tuple-element.352.refs_0_, s32[16]{0:T(128)S(1)} %get-tuple-element.351.refs_1_.refs_2_, s32[4,8]{1,0:T(4,128)S(1)} %get-tuple-element.353.refs_2_.refs_3_, s32[4,8]{1,0:T(4,128)S(1)} %get-tuple-element.354.refs_3_.refs_4_, ...), custom_call_target="tpu_custom_call" | custom-call | flops 3221225472 | tf_op jit(solution)/shard_map/cond/branch_1_fun/left_products/pallas_call | solution.py:157
  54.6 2.9 %right_products.19 = (f32[512,256]{1,0:T(8,128)S(1)}, f32[512,256]{1,0:T(8,128)}) custom-call(s32[2]{0:T(128)S(1)} %get-tuple-element.352.refs_0_, s32[16]{0:T(128)S(1)} %get-tuple-element.351.refs_1_.refs_2_, s32[16]{0:T(128)S(1)} %get-tuple-element.351.refs_1_.refs_2_, s32[4,8]{1,0:T(4,128)S(1)} %get-tuple-element.353.refs_2_.refs_3_, ...), custom_call_target="tpu_custom_call" | custom-call | flops 805306368 | tf_op jit(solution)/shard_map/cond/branch_1_fun/right_products/pallas_call | solution.py:287
  57.5 3.7 %left_products.18.refs_5_ = bf16[1,2,512,512]{3,2,1,0:T(8,128)(2,1)S(1)} custom-call(s32[2]{0:T(128)S(1)} %get-tuple-element.352.refs_0_, s32[16]{0:T(128)S(1)} %get-tuple-element.351.refs_1_.refs_2_, s32[4,8]{1,0:T(4,128)S(1)} %get-tuple-element.353.refs_2_.refs_3_, s32[4,8]{1,0:T(4,128)S(1)} %get-tuple-element.354.refs_3_.refs_4_, ...), custom_call_target="tpu_custom_call" | custom-call | flops 1610612736 | tf_op jit(solution)/shard_map/cond/branch_1_fun/left_products/pallas_call | solution.py:157
  61.2 1.4 right_products.18
  62.6 9.6 %collective-permute-done.2 = f32[512,256]{1,0:T(8,128)} collective-permute-done((f32[512,256]{1,0:T(8,128)S(1)}, f32[512,256]{1,0:T(8,128)}, u32[]{:S(2)}, u32[]{:S(2)}) %collective-permute-start.2) | collective-permute-done | bytes 524320 | tf_op jit(solution)/shard_map/cond/branch_1_fun/ppermute | solution.py:422
  81.2 2.6 %collective-permute-start.26 = (f32[512,256]{1,0:T(8,128)S(1)}, f32[512,256]{1,0:T(8,128)S(1)}, u32[]{:S(2)}, u32[]{:S(2)}) collective-permute-start(f32[512,256]{1,0:T(8,128)S(1)} %add.6.refs_0_.refs_9_), channel_id=1, source_target_pairs={{0,2},{1,3},{2,0},{3,1},{4,6},{5,7},{6,4},{7,5},{8,10},{9,11},{10,... | collective-permute-start | bytes 1572872 | tf_op jit(solution)/shard_map/ppermute | solution.py:422
  83.7 20.1 %conditional.4 = (f32[512,256]{1,0:T(8,128)}, s32[1]{0:T(128)}, f32[3,256,256]{2,1,0:T(8,128)}, f32[256,256]{1,0:T(8,128)S(1)}) conditional(s32[]{:T(128)} %bitcast.4, (f32[512,256]{1,0:T(8,128)S(1)}, s32[2]{0:T(128)S(1)}, s32[16]{0:T(128)S(1)}, s32[4,8]{1,0:T(4,128)S(1)}, s32[4,8]{1,0:T(4,128)S(1)}, ...), branch_computations={%region_3.0_spmd, %region_4.0_spmd, %region_5.0_spmd} | conditional | flops 4026531840 | bytes 12583124 | solution.py:470
  83.8 5.6 %left_products.23.refs_5_ = bf16[2,2,512,512]{3,2,1,0:T(8,128)(2,1)S(1)} custom-call(s32[2]{0:T(128)S(1)} %get-tuple-element.398.refs_0_, s32[16]{0:T(128)S(1)} %get-tuple-element.399.refs_1_, s32[4,8]{1,0:T(4,128)S(1)} %get-tuple-element.401.refs_2_.refs_3_, s32[4,8]{1,0:T(4,128)S(1)} %get-tuple-element.402.refs_3_.refs_4_, ...), custom_call_target="tpu_custom_call" | custom-call | flops 3221225472 | tf_op jit(solution)/shard_map/cond/branch_1_fun/left_products/pallas_call | solution.py:157
  89.5 3.1 %right_products.23 = (s32[1]{0:T(128)}, f32[3,256,256]{2,1,0:T(8,128)}, f32[256,256]{1,0:T(8,128)S(1)}) custom-call(s32[2]{0:T(128)S(1)} %get-tuple-element.398.refs_0_, s32[16]{0:T(128)S(1)} %get-tuple-element.399.refs_1_, s32[16]{0:T(128)} %get-tuple-element.400.refs_2_, s32[4,8]{1,0:T(4,128)S(1)} %get-tuple-element.401.refs_2_.refs_3_, ...), custom_call_target="tpu_custom_call" | custom-call | flops 805306368 | tf_op jit(solution)/shard_map/cond/branch_1_fun/right_products/pallas_call | solution.py:287
  92.6 11.3 %collective-permute-done.7 = f32[512,256]{1,0:T(8,128)} collective-permute-done((f32[512,256]{1,0:T(8,128)S(1)}, f32[512,256]{1,0:T(8,128)}, u32[]{:S(2)}, u32[]{:S(2)}) %collective-permute-start.7) | collective-permute-done | bytes 524320 | tf_op jit(solution)/shard_map/cond/branch_1_fun/ppermute | solution.py:422
  103.9 1.3 add.7.refs_4_.refs_14_
  105.3 2.6 %collective-permute-start.29 = (f32[512,256]{1,0:T(8,128)S(1)}, f32[512,256]{1,0:T(8,128)}, u32[]{:S(2)}, u32[]{:S(2)}) collective-permute-start(f32[512,256]{1,0:T(8,128)S(1)} %add.7.refs_4_.refs_14_), channel_id=1, source_target_pairs={{0,2},{1,3},{2,0},{3,1},{4,6},{5,7},{6,4},{7,5},{8,10},{9,11},{10,... | collective-permute-start | bytes 1572872 | tf_op jit(solution)/shard_map/ppermute | solution.py:422
  108.5 37.7 %conditional.5 = (f32[3,256,256]{2,1,0:T(8,128)}, f32[256,256]{1,0:T(8,128)S(1)}, f32[512,512]{1,0:T(8,128)S(1)}) conditional(s32[]{:T(128)} %bitcast.9, (f32[3,256,256]{2,1,0:T(8,128)}, s32[2]{0:T(128)S(1)}, s32[16]{0:T(128)S(1)}, s32[4,8]{1,0:T(4,128)S(1)}, s32[4,8]{1,0:T(4,128)S(1)}, ...), branch_computations={%region_6.0_spmd, %region_7.0_spmd, %region_8.0_spmd, %region_9.0_... | conditional | flops 4026531840 | bytes 15204596 | solution.py:470
  108.8 5.7 %left_products.27.refs_5_ = bf16[2,2,512,512]{3,2,1,0:T(8,128)(2,1)S(1)} custom-call(s32[2]{0:T(128)S(1)} %get-tuple-element.461.refs_0_, s32[16]{0:T(128)S(1)} %get-tuple-element.462.refs_1_.refs_2_, s32[4,8]{1,0:T(4,128)S(1)} %get-tuple-element.463.refs_2_.refs_3_, s32[4,8]{1,0:T(4,128)S(1)} %get-tuple-element.464.refs_3_.refs_4_, ...), custom_call_target="tpu_custom_call" | custom-call | flops 3221225472 | tf_op jit(solution)/shard_map/cond/branch_2_fun/left_products/pallas_call | solution.py:157
  114.6 2.1 %right_products.27 = f32[512,512]{1,0:T(8,128)S(1)} custom-call(s32[2]{0:T(128)S(1)} %get-tuple-element.461.refs_0_, s32[16]{0:T(128)S(1)} %get-tuple-element.462.refs_1_.refs_2_, s32[16]{0:T(128)S(1)} %get-tuple-element.462.refs_1_.refs_2_, s32[4,8]{1,0:T(4,128)S(1)} %get-tuple-element.463.refs_2_.refs_3_, s32[4,8]{1,0:T(4,128)S(1)} %get-tuple-element.464.refs_3_.refs_4_, ...), custom_call_target="tpu_custom_call" | custom-call | flops 805306368 | tf_op jit(solution)/shard_map/cond/branch_2_fun/right_products/pallas_call | solution.py:287
  116.7 29.2 %collective-permute-done.12 = f32[3,256,256]{2,1,0:T(8,128)} collective-permute-done((f32[3,256,256]{2,1,0:T(8,128)}, f32[3,256,256]{2,1,0:T(8,128)}, u32[]{:S(2)}, u32[]{:S(2)}) %collective-permute-start.12) | collective-permute-done | bytes 786464 | tf_op jit(solution)/shard_map/cond/branch_2_fun/ppermute | solution.py:422
  146.2 3.0 %wished.1 = f32[2,512,256]{2,1,0:T(8,128)S(1)} custom-call(s32[1]{0:T(128)} %get-tuple-element.580.wish, f32[512,256]{1,0:T(8,128)S(1)} %add.6.refs_0_.refs_9_, f32[512,256]{1,0:T(8,128)S(1)} %collective-permute-done.26.refs_1_.refs_10_, f32[512,256]{1,0:T(8,128)S(1)} %collective-permute-done.27.refs_2_.refs_11_, ...), custom_call_target="tpu_custom_call" | custom-call | tf_op jit(solution)/shard_map/wished/pallas_call | solution.py:406
  149.2 2.6 %collective-permute-done.32.refs_8_.refs_13_ = f32[2,512,256]{2,1,0:T(8,128)S(1)} collective-permute-done((f32[2,512,256]{2,1,0:T(8,128)S(1)}, f32[2,512,256]{2,1,0:T(8,128)S(1)}, u32[]{:S(2)}, u32[]{:S(2)}) %collective-permute-start.32) | collective-permute-done | bytes 1048608 | tf_op jit(solution)/shard_map/ppermute | solution.py:422
  151.9 4.8 %sum_blocks.1 = f32[512,512]{1,0:T(8,128)} custom-call(s32[2]{0:T(128)S(1)} %pad_add_fusion.me.refs_0_, s32[16]{0:T(128)S(1)} %get-tuple-element.553.refs_1_.refs_2_, s32[16]{0:T(128)} %get-tuple-element.562.refs_2_, s32[4,8]{1,0:T(4,128)S(1)} %bitcast.25, s32[4,8]{1,0:T(4,128)S(1)} %copy-done.53, f32[512,512]{1,0:T(8,128)S(1)} %get-tuple-element.575.refs_5_, ...), custom_call_target="tpu_custom_call" | custom-call | tf_op jit(solution)/shard_map/sum_blocks/pallas_call | solution.py:364
  (64 shorter events, 6.6 us)
Async XLA Ops:
  0.0 29.7 %copy-start.2 = (f32[512,256]{1,0:T(8,128)S(1)}, f32[512,256]{1,0:T(8,128)}, u32[]{:S(2)}) copy-start(f32[512,256]{1,0:T(8,128)} %refs_6_.1) | copy-start | bytes 1572868
  0.0 32.3 %copy-start.53 = (s32[4,8]{1,0:T(4,128)S(1)}, s32[4,8]{1,0:T(4,128)}, u32[]{:S(2)}) copy-start(s32[4,8]{1,0:T(4,128)} %refs_4_.5) | copy-start | bytes 388
  0.0 32.3 %copy-start.52 = (s32[8,4]{0,1:T(4,128)S(1)}, s32[8,4]{0,1:T(4,128)}, u32[]{:S(2)}) copy-start(s32[8,4]{0,1:T(4,128)} %param.24) | copy-start | bytes 388
  0.0 7.5 %collective-permute-start.18 = (f32[256,256]{1,0:T(8,128)}, f32[256,256]{1,0:T(8,128)S(1)}, u32[]{:S(2)}, u32[]{:S(2)}) collective-permute-start(f32[256,256]{1,0:T(8,128)} %param.22), channel_id=1, source_target_pairs={{0,2},{1,3},{2,0},{3,1},{4,6},{5,7},{6,4},{7,5},{8,10},{9,11},{10,... | collective-permute-start | bytes 786440 | tf_op jit(solution)/shard_map/ppermute | solution.py:422
  0.1 24.2 %collective-permute-start.22 = (f32[512,256]{1,0:T(8,128)}, f32[512,256]{1,0:T(8,128)S(1)}, u32[]{:S(2)}, u32[]{:S(2)}) collective-permute-start(f32[512,256]{1,0:T(8,128)} %refs_6_.1), channel_id=1, source_target_pairs={{0,8},{8,0},{16,24},{24,16},{1,9},{9,1},{17,25},{25,17},{2,10},{10... | collective-permute-start | bytes 1572872 | tf_op jit(solution)/shard_map/ppermute | solution.py:422
  1.6 22.6 %collective-permute-start.21 = (f32[512,256]{1,0:T(8,128)}, f32[512,256]{1,0:T(8,128)S(1)}, u32[]{:S(2)}, u32[]{:S(2)}) collective-permute-start(f32[512,256]{1,0:T(8,128)} %refs_6_.1), channel_id=1, source_target_pairs={{0,16},{8,24},{16,0},{24,8},{1,17},{9,25},{17,1},{25,9},{2,18},{10... | collective-permute-start | bytes 1572872 | tf_op jit(solution)/shard_map/ppermute | solution.py:422
  3.9 6.5 %collective-permute-start.19 = (f32[256,256]{1,0:T(8,128)}, f32[256,256]{1,0:T(8,128)S(1)}, u32[]{:S(2)}, u32[]{:S(2)}) collective-permute-start(f32[256,256]{1,0:T(8,128)} %param.22), channel_id=1, source_target_pairs={{0,4},{1,5},{2,6},{3,7},{4,0},{5,1},{6,2},{7,3},{8,12},{9,13},{10,... | collective-permute-start | bytes 786440 | tf_op jit(solution)/shard_map/ppermute | solution.py:422
  7.5 8.6 %collective-permute-start.20 = (f32[256,256]{1,0:T(8,128)S(1)}, f32[256,256]{1,0:T(8,128)S(1)}, u32[]{:S(2)}, u32[]{:S(2)}) collective-permute-start(f32[256,256]{1,0:T(8,128)S(1)} %collective-permute-done.18), channel_id=1, source_target_pairs={{0,4},{1,5},{2,6},{3,7},{4,0},{5,1},{6,2},{7,3},{8,12},{9,13},{10,... | collective-permute-start | bytes 786440 | tf_op jit(solution)/shard_map/ppermute | solution.py:422
  24.3 22.9 %copy-start.12 = (f32[512,256]{1,0:T(8,128)}, f32[512,256]{1,0:T(8,128)S(1)}, u32[]{:S(2)}) copy-start(f32[512,256]{1,0:T(8,128)S(1)} %collective-permute-done.22.refs_7_) | copy-start | bytes 1572868
  24.3 22.9 %copy-start.22 = (f32[512,256]{1,0:T(8,128)}, f32[512,256]{1,0:T(8,128)S(1)}, u32[]{:S(2)}) copy-start(f32[512,256]{1,0:T(8,128)S(1)} %collective-permute-done.21.refs_8_) | copy-start | bytes 1572868
  25.5 58.2 %copy-start = (f32[4,256,256]{2,1,0:T(8,128)}, f32[4,256,256]{2,1,0:T(8,128)S(1)}, u32[]{:S(2)}) copy-start(f32[4,256,256]{2,1,0:T(8,128)S(1)} %pad_maximum_fusion.refs_5_) | copy-start | bytes 3145732
  25.5 6.8 %collective-permute-start.23 = (f32[4,256,256]{2,1,0:T(8,128)S(1)}, f32[4,256,256]{2,1,0:T(8,128)S(1)}, u32[]{:S(2)}, u32[]{:S(2)}) collective-permute-start(f32[4,256,256]{2,1,0:T(8,128)S(1)} %pad_maximum_fusion.refs_5_), channel_id=1, source_target_pairs={{0,1},{1,0},{2,3},{3,2},{4,5},{5,4},{6,7},{7,6},{8,9},{9,8},{10,11... | collective-permute-start | bytes 3145736 | tf_op jit(solution)/shard_map/ppermute | solution.py:422
  29.7 6.4 %collective-permute-start.24 = (f32[512,256]{1,0:T(8,128)S(1)}, f32[512,256]{1,0:T(8,128)S(1)}, u32[]{:S(2)}, u32[]{:S(2)}) collective-permute-start(f32[512,256]{1,0:T(8,128)S(1)} %copy-done.2), channel_id=1, source_target_pairs={{8,16},{16,8},{9,17},{17,9},{10,18},{18,10},{11,19},{19,11},{12,20... | collective-permute-start | bytes 1572872 | tf_op jit(solution)/shard_map/ppermute | solution.py:429
  30.3 15.4 %collective-permute-start.25 = (f32[512,256]{1,0:T(8,128)S(1)}, f32[512,256]{1,0:T(8,128)S(1)}, u32[]{:S(2)}, u32[]{:S(2)}) collective-permute-start(f32[512,256]{1,0:T(8,128)S(1)} %collective-permute-done.21.refs_8_), channel_id=1, source_target_pairs={{8,0},{16,24},{9,1},{17,25},{10,2},{18,26},{11,3},{19,27},{12,4},{... | collective-permute-start | bytes 1572872 | tf_op jit(solution)/shard_map/ppermute | solution.py:438
  32.3 14.8 %copy-start.1 = (f32[4,256,256]{2,1,0:T(8,128)}, f32[4,256,256]{2,1,0:T(8,128)S(1)}, u32[]{:S(2)}) copy-start(f32[4,256,256]{2,1,0:T(8,128)S(1)} %collective-permute-done.23.refs_6_) | copy-start | bytes 3145732
  36.0 11.1 %copy-start.32 = (f32[512,256]{1,0:T(8,128)}, f32[512,256]{1,0:T(8,128)S(1)}, u32[]{:S(2)}) copy-start(f32[512,256]{1,0:T(8,128)S(1)} %collective-permute-done.24.refs_9_) | copy-start | bytes 1572868
  47.2 15.4 %collective-permute-start.3 = (s32[16]{0:T(128)S(1)}, s32[16]{0:T(128)}, u32[]{:S(2)}, u32[]{:S(2)}) collective-permute-start(s32[16]{0:T(128)S(1)} %get-tuple-element.351.refs_1_.refs_2_), channel_id=1, source_target_pairs={{0,16},{8,24},{16,0},{24,8},{1,17},{9,25},{17,1},{25,9},{2,18},{10... | collective-permute-start | bytes 200 | tf_op jit(solution)/shard_map/cond/branch_1_fun/ppermute | solution.py:422
  47.5 24.7 %collective-permute-start.2 = (f32[512,256]{1,0:T(8,128)S(1)}, f32[512,256]{1,0:T(8,128)}, u32[]{:S(2)}, u32[]{:S(2)}) collective-permute-start(f32[512,256]{1,0:T(8,128)S(1)} %get-tuple-element.350), channel_id=1, source_target_pairs={{0,16},{8,24},{16,0},{24,8},{1,17},{9,25},{17,1},{25,9},{2,18},{10... | collective-permute-start | bytes 1572872 | tf_op jit(solution)/shard_map/cond/branch_1_fun/ppermute | solution.py:422
  81.0 22.9 %collective-permute-start.28 = (f32[512,256]{1,0:T(8,128)S(1)}, f32[512,256]{1,0:T(8,128)S(1)}, u32[]{:S(2)}, u32[]{:S(2)}) collective-permute-start(f32[512,256]{1,0:T(8,128)S(1)} %add.6.refs_0_.refs_9_), channel_id=1, source_target_pairs={{0,6},{1,7},{2,4},{3,5},{4,2},{5,3},{6,0},{7,1},{8,14},{9,15},{10,... | collective-permute-start | bytes 1572872 | tf_op jit(solution)/shard_map/ppermute | solution.py:422
  81.1 22.8 %collective-permute-start.27 = (f32[512,256]{1,0:T(8,128)S(1)}, f32[512,256]{1,0:T(8,128)S(1)}, u32[]{:S(2)}, u32[]{:S(2)}) collective-permute-start(f32[512,256]{1,0:T(8,128)S(1)} %add.6.refs_0_.refs_9_), channel_id=1, source_target_pairs={{0,4},{1,5},{2,6},{3,7},{4,0},{5,1},{6,2},{7,3},{8,12},{9,13},{10,... | collective-permute-start | bytes 1572872 | tf_op jit(solution)/shard_map/ppermute | solution.py:422
  81.2 22.7 %collective-permute-start.26 = (f32[512,256]{1,0:T(8,128)S(1)}, f32[512,256]{1,0:T(8,128)S(1)}, u32[]{:S(2)}, u32[]{:S(2)}) collective-permute-start(f32[512,256]{1,0:T(8,128)S(1)} %add.6.refs_0_.refs_9_), channel_id=1, source_target_pairs={{0,2},{1,3},{2,0},{3,1},{4,6},{5,7},{6,4},{7,5},{8,10},{9,11},{10,... | collective-permute-start | bytes 1572872 | tf_op jit(solution)/shard_map/ppermute | solution.py:422
  83.7 20.1 %collective-permute-start.7 = (f32[512,256]{1,0:T(8,128)S(1)}, f32[512,256]{1,0:T(8,128)}, u32[]{:S(2)}, u32[]{:S(2)}) collective-permute-start(f32[512,256]{1,0:T(8,128)S(1)} %get-tuple-element.397), channel_id=1, source_target_pairs={{0,16},{8,24},{16,0},{24,8},{1,17},{9,25},{17,1},{25,9},{2,18},{10... | collective-permute-start | bytes 1572872 | tf_op jit(solution)/shard_map/cond/branch_1_fun/ppermute | solution.py:422
  105.1 41.0 %collective-permute-start.31 = (f32[512,256]{1,0:T(8,128)S(1)}, f32[512,256]{1,0:T(8,128)S(1)}, u32[]{:S(2)}, u32[]{:S(2)}) collective-permute-start(f32[512,256]{1,0:T(8,128)S(1)} %add.7.refs_4_.refs_14_), channel_id=1, source_target_pairs={{0,6},{1,7},{2,4},{3,5},{4,2},{5,3},{6,0},{7,1},{8,14},{9,15},{10,... | collective-permute-start | bytes 1572872 | tf_op jit(solution)/shard_map/ppermute | solution.py:422
  105.2 41.0 %collective-permute-start.30 = (f32[512,256]{1,0:T(8,128)S(1)}, f32[512,256]{1,0:T(8,128)}, u32[]{:S(2)}, u32[]{:S(2)}) collective-permute-start(f32[512,256]{1,0:T(8,128)S(1)} %add.7.refs_4_.refs_14_), channel_id=1, source_target_pairs={{0,4},{1,5},{2,6},{3,7},{4,0},{5,1},{6,2},{7,3},{8,12},{9,13},{10,... | collective-permute-start | bytes 1572872 | tf_op jit(solution)/shard_map/ppermute | solution.py:422
  105.3 40.9 %collective-permute-start.29 = (f32[512,256]{1,0:T(8,128)S(1)}, f32[512,256]{1,0:T(8,128)}, u32[]{:S(2)}, u32[]{:S(2)}) collective-permute-start(f32[512,256]{1,0:T(8,128)S(1)} %add.7.refs_4_.refs_14_), channel_id=1, source_target_pairs={{0,2},{1,3},{2,0},{3,1},{4,6},{5,7},{6,4},{7,5},{8,10},{9,11},{10,... | collective-permute-start | bytes 1572872 | tf_op jit(solution)/shard_map/ppermute | solution.py:422
  108.7 37.2 %collective-permute-start.12 = (f32[3,256,256]{2,1,0:T(8,128)}, f32[3,256,256]{2,1,0:T(8,128)}, u32[]{:S(2)}, u32[]{:S(2)}) collective-permute-start(f32[3,256,256]{2,1,0:T(8,128)} %get-tuple-element.459), channel_id=1, source_target_pairs={{0,16},{8,24},{16,0},{24,8},{1,17},{9,25},{17,1},{25,9},{2,18},{10... | collective-permute-start | bytes 2359304 | tf_op jit(solution)/shard_map/cond/branch_2_fun/ppermute | solution.py:422
  108.8 5.7 %copy-start.8 = (f32[512,256]{1,0:T(8,128)S(1)}, f32[512,256]{1,0:T(8,128)}, u32[]{:S(2)}) copy-start(f32[512,256]{1,0:T(8,128)} %get-tuple-element.468.refs_6_) | copy-start | bytes 1572868 | tf_op jit(solution)/shard_map/cond
  108.8 5.7 %copy-start.18 = (f32[512,256]{1,0:T(8,128)S(1)}, f32[512,256]{1,0:T(8,128)}, u32[]{:S(2)}) copy-start(f32[512,256]{1,0:T(8,128)} %get-tuple-element.469.refs_7_) | copy-start | bytes 1572868 | tf_op jit(solution)/shard_map/cond
  108.8 5.7 %copy-start.28 = (f32[512,256]{1,0:T(8,128)S(1)}, f32[512,256]{1,0:T(8,128)}, u32[]{:S(2)}) copy-start(f32[512,256]{1,0:T(8,128)} %get-tuple-element.470.refs_8_) | copy-start | bytes 1572868 | tf_op jit(solution)/shard_map/cond
  108.8 5.7 %copy-start.38 = (f32[512,256]{1,0:T(8,128)S(1)}, f32[512,256]{1,0:T(8,128)}, u32[]{:S(2)}) copy-start(f32[512,256]{1,0:T(8,128)} %get-tuple-element.471.refs_9_) | copy-start | bytes 1572868 | tf_op jit(solution)/shard_map/cond
  108.8 5.7 %copy-start.48 = (f32[512,256]{1,0:T(8,128)S(1)}, f32[512,256]{1,0:T(8,128)}, u32[]{:S(2)}) copy-start(f32[512,256]{1,0:T(8,128)} %get-tuple-element.472.refs_10_) | copy-start | bytes 1572868 | tf_op jit(solution)/shard_map/cond
  149.2 2.7 %collective-permute-start.32 = (f32[2,512,256]{2,1,0:T(8,128)S(1)}, f32[2,512,256]{2,1,0:T(8,128)S(1)}, u32[]{:S(2)}, u32[]{:S(2)}) collective-permute-start(f32[2,512,256]{2,1,0:T(8,128)S(1)} %wished.1), channel_id=1, source_target_pairs={{0,1},{1,0},{2,3},{3,2},{4,5},{5,4},{6,7},{7,6},{8,9},{9,8},{10,11... | collective-permute-start | bytes 3145736 | tf_op jit(solution)/shard_map/ppermute | solution.py:422
  (6 other events, 29.9 us)

commit v3 on v1

--- a/solution.py
+++ b/solution.py
@@ -74,24 +74,27 @@
 
 
 class Columns:
-    ON, REST, KEPT = range(3)
+    FIRST, NEXT, REST, KEPT = range(4)
 
     def __init__(self, kind, block_cols):
         self.kind = kind
         self.given = kind != self.KEPT
         self.half_cols = block_cols // 2
-        self.steps = block_cols if kind == self.KEPT else self.half_cols
+        self.skip = 1 if kind == self.NEXT else 0
+        self.steps = 1 if kind == self.FIRST else self.half_cols - self.skip
+        if kind == self.KEPT:
+            self.steps = block_cols
 
     def half(self, step, me, row_partner, col_partner):
+        holder = row_partner[me[0], me[1]] if self.given else me[0]
+        goes_on = (me[1] < col_partner[holder, me[1]]).astype(jnp.int32)
         if self.kind == self.KEPT:
-            goes_on = (me[1] < col_partner[me[0], me[1]]).astype(jnp.int32)
             return goes_on ^ div(step, self.half_cols)
-        goes_on = (me[1] < col_partner[row_partner[me[0], me[1]], me[1]]).astype(jnp.int32)
         return goes_on ^ (1 if self.kind == self.REST else 0)
 
     def column(self, step, me, row_partner, col_partner):
         half = self.half(step, me, row_partner, col_partner)
-        return half * self.half_cols + rem(step, self.half_cols)
+        return half * self.half_cols + self.skip + rem(step, self.half_cols)
 
 
 def left_kernel(columns, block_cols, half_rows, per_step, *refs):
@@ -209,18 +212,19 @@
 
     @pl.when(step == 0)
     def _():
-        half = columns.half(step, me, row_partner, col_partner)
+        low = columns.column(0, me, row_partner, col_partner) * tile_order
         for (start, filled), piece in zip(starts, pieces):
-            wanted = start(me) >= 0
+            begin = start(me)
+            wanted = begin >= 0
             if columns.given:
-                wanted = div(start(me), columns.half_cols * tile_order) == half
+                wanted = (begin < low + columns.steps * tile_order) & (begin + piece.shape[0] > low)
             if filled is not None:
                 wanted &= filled(me)
 
             @pl.when(wanted)
             def _():
                 depth = piece.shape[0]
-                rows = pl.ds(pl.multiple_of(start(me), depth), depth)
+                rows = pl.ds(pl.multiple_of(begin, depth), depth)
                 p_high[rows, :], p_low[rows, :] = split(piece[...])
 
     column = columns.column(step, me, row_partner, col_partner)
@@ -280,8 +284,9 @@
         out_specs += [pl.BlockSpec(shape, lambda i, *_, n=len(shape): (0,) * n) for shape in shapes]
         scratch = [pltpu.VMEM((blocks, width, width), F32)] + scratch
     else:
-        shapes = [(height, width)] * half_cols
-        out_specs = [pl.BlockSpec((height, width), lambda i, *_: (0, 0))] * half_cols
+        count = min(columns.steps, half_cols)
+        shapes = [(height, width)] * count
+        out_specs = [pl.BlockSpec((height, width), lambda i, *_: (0, 0))] * count
         if kind == Columns.KEPT:
             shapes += [(height, half_cols * width)]
             out_specs += [
@@ -510,8 +515,8 @@
             return right_products(kind, tables, w, shards, half_rows, block_cols)
 
         def swap_first(mask, _, chunk):
-            received = flip(chunk, "row", n_row, mask)
-            return received, flip(slots, "row", n_row, mask), products(Columns.KEPT, slots)
+            received = flip(chunk, "row", n_row, mask), flip(slots, "row", n_row, mask)
+            return *received, products(Columns.NEXT, slots), products(Columns.KEPT, slots)
 
         def swap_next(mask, _, operands):
             chunk, mate_slots = operands
@@ -526,8 +531,9 @@
                 for index, array in enumerate(rest)
             ]
 
-        given = products(Columns.ON, slots)
-        received, mate_slots, kept = pair_switch(first, n_row, swap_first, given[0])
+        given = products(Columns.FIRST, slots)
+        received, mate_slots, others, kept = pair_switch(first, n_row, swap_first, given[0])
+        given = [*given, *others]
         sections, rest = [], None
         for index in range(half_cols):
             section = kept[index] + received

time: 162 us -> 167 us (1.031)
  the two profiles are of different devices: /device:TPU:7 before, /device:TPU:3 now
where the time goes in v3:
time: 167 us; the launch traced here: 166 us
  waiting for transfers between devices  94.2 us (56%)
  Pallas kernels  44.3 us (27%)
  starting transfers between devices  21.1 us (13%)
  other arithmetic  3.65 us (2%)
  between operations  2.14 us (1%)
    ppermute x18, waiting for transfers between devices, flip(): return lax.ppermute(value, axis, [(i, i ^ mask) for i in range(size)])  84.4 us
    pallas_call x4, Pallas kernels, left_products(): pl.pallas_call(functools.partial(left_kernel, columns, block_cols, half_r...  20.6 us
    ppermute x18, starting transfers between devices, flip(): return lax.ppermute(value, axis, [(i, i ^ mask) for i in range(size)])  18.3 us
    pallas_call x4, Pallas kernels, right_products(): pl.pallas_call(functools.partial(right_kernel, columns, block_cols, half_...  15.4 us
    ppermute x1, waiting for transfers between devices, gather_prolong(): handed = lax.ppermute(by_two, axis, [(1, 0), (2, 3)])  9.77 us
    pallas_call x1, Pallas kernels, sum_blocks(): pl.pallas_call(functools.partial(sum_kernel, half_rows, block_cols, len(s...  4.71 us
  transfers between devices with their start and end apart: 20, of which 9 were waited for; matrix products, arithmetic and copies ran while one was open for 0% of the time, Pallas kernels for 21%

profile of v3, /device:TPU:3, one launch (start us, length us, event | category | flops | bytes accessed | tf_op | source)
XLA Modules:
  0.0 165.6 jit_solution(6067429855456051421)
XLA Ops:
  0.0 2.6 %collective-permute-start.21 = (f32[512,256]{1,0:T(8,128)}, f32[512,256]{1,0:T(8,128)}, u32[]{:S(2)}, u32[]{:S(2)}) collective-permute-start(f32[512,256]{1,0:T(8,128)} %refs_6_.1), channel_id=1, source_target_pairs={{0,16},{8,24},{16,0},{24,8},{1,17},{9,25},{17,1},{25,9},{2,18},{10... | collective-permute-start | bytes 1572872 | tf_op jit(solution)/shard_map/ppermute | solution.py:433
  2.6 1.3 collective-permute-start.22
  3.9 1.2 collective-permute-start.19
  5.8 1.4 make_tables.1
  8.6 1.8 %collective-permute-done.19 = f32[256,256]{1,0:T(8,128)S(1)} collective-permute-done((f32[256,256]{1,0:T(8,128)}, f32[256,256]{1,0:T(8,128)S(1)}, u32[]{:S(2)}, u32[]{:S(2)}) %collective-permute-start.19) | collective-permute-done | bytes 262176 | tf_op jit(solution)/shard_map/ppermute | solution.py:433
  10.5 5.6 %collective-permute-done.20 = f32[256,256]{1,0:T(8,128)S(1)} collective-permute-done((f32[256,256]{1,0:T(8,128)S(1)}, f32[256,256]{1,0:T(8,128)S(1)}, u32[]{:S(2)}, u32[]{:S(2)}) %collective-permute-start.20) | collective-permute-done | bytes 262176 | tf_op jit(solution)/shard_map/ppermute | solution.py:433
  16.1 9.4 %collective-permute-done.21.refs_8_ = f32[512,256]{1,0:T(8,128)} collective-permute-done((f32[512,256]{1,0:T(8,128)}, f32[512,256]{1,0:T(8,128)}, u32[]{:S(2)}, u32[]{:S(2)}) %collective-permute-start.21) | collective-permute-done | bytes 524320 | tf_op jit(solution)/shard_map/ppermute | solution.py:433
  26.7 1.7 %collective-permute-start.23 = (f32[4,256,256]{2,1,0:T(8,128)S(1)}, f32[4,256,256]{2,1,0:T(8,128)S(1)}, u32[]{:S(2)}, u32[]{:S(2)}) collective-permute-start(f32[4,256,256]{2,1,0:T(8,128)S(1)} %pad_maximum_fusion.refs_5_), channel_id=1, source_target_pairs={{0,1},{1,0},{2,3},{3,2},{4,5},{5,4},{6,7},{7,6},{8,9},{9,8},{10,11... | collective-permute-start | bytes 3145736 | tf_op jit(solution)/shard_map/ppermute | solution.py:433
  28.5 1.5 collective-permute-start.24
  29.9 1.3 collective-permute-start.25
  31.9 3.9 %left_products.19.refs_5_ = bf16[1,2,512,512]{3,2,1,0:T(8,128)(2,1)S(1)} custom-call(s32[2]{0:T(128)S(1)} %pad_add_fusion.me.refs_0_, s32[16]{0:T(128)S(1)} %get-tuple-element.340.refs_1_.refs_2_, s32[4,8]{1,0:T(4,128)} %bitcast.11, s32[4,8]{1,0:T(4,128)} %refs_4_.5, f32[16,512,512]{2,1,0:T(8,128)} %refs_4_.3, f32[4,256,256]{2,1,0:T(8,128)S(1)} %pad_maximum_fusion.refs_5_, ...), custom_call_target="tpu_custom_call" | custom-call | flops 1610612736 | tf_op jit(solution)/shard_map/left_products/pallas_call | solution.py:162
  35.9 9.8 %collective-permute-done.25.refs_10_ = f32[512,256]{1,0:T(8,128)} collective-permute-done((f32[512,256]{1,0:T(8,128)}, f32[512,256]{1,0:T(8,128)}, u32[]{:S(2)}, u32[]{:S(2)}) %collective-permute-start.25) | collective-permute-done | bytes 524320 | tf_op jit(solution)/shard_map/ppermute | solution.py:449
  45.7 2.7 %right_products.19 = f32[512,256]{1,0:T(8,128)S(1)} custom-call(s32[2]{0:T(128)S(1)} %pad_add_fusion.me.refs_0_, s32[16]{0:T(128)S(1)} %get-tuple-element.340.refs_1_.refs_2_, s32[16]{0:T(128)S(1)} %get-tuple-element.340.refs_1_.refs_2_, s32[4,8]{1,0:T(4,128)S(1)} %bitcast.12, s32[4,8]{1,0:T(4,128)S(1)} %copy-done.11, ...), custom_call_target="tpu_custom_call" | custom-call | flops 402653184 | tf_op jit(solution)/shard_map/right_products/pallas_call | solution.py:298
  48.4 26.3 %conditional.3 = (f32[512,256]{1,0:T(8,128)}, s32[16]{0:T(128)}, f32[512,256]{1,0:T(8,128)S(1)}, f32[512,256]{1,0:T(8,128)S(1)}, f32[512,256]{1,0:T(8,128)}, /*index=5*/f32[512,512]{1,0:T(8,128)}) conditional(s32[]{:T(128)} %bitcast.4, (f32[512,256]{1,0:T(8,128)S(1)}, s32[16]{0:T(128)S(1)}, s32[2]{0:T(128)S(1)}, ...), branch_computations={%region_0.0_spmd, %region_1.0_spmd, %region_2.0_spmd} | conditional | flops 10066329600 | bytes 2097536 | solution.py:481
  50.8 7.7 %left_products.13.refs_5_ = bf16[4,2,512,512]{3,2,1,0:T(8,128)(2,1)S(1)} custom-call(s32[2]{0:T(128)S(1)} %get-tuple-element.209.refs_0_, s32[16]{0:T(128)S(1)} %get-tuple-element.208.refs_1_.refs_2_, s32[4,8]{1,0:T(4,128)S(1)} %get-tuple-element.210.refs_2_.refs_3_, s32[4,8]{1,0:T(4,128)S(1)} %get-tuple-element.211.refs_3_.refs_4_, ...), custom_call_target="tpu_custom_call" | custom-call | flops 6442450944 | tf_op jit(solution)/shard_map/cond/branch_1_fun/left_products/pallas_call | solution.py:162
  58.5 3.7 %left_products.12.refs_5_ = bf16[1,2,512,512]{3,2,1,0:T(8,128)(2,1)S(1)} custom-call(s32[2]{0:T(128)S(1)} %get-tuple-element.209.refs_0_, s32[16]{0:T(128)S(1)} %get-tuple-element.208.refs_1_.refs_2_, s32[4,8]{1,0:T(4,128)S(1)} %get-tuple-element.210.refs_2_.refs_3_, s32[4,8]{1,0:T(4,128)S(1)} %get-tuple-element.211.refs_3_.refs_4_, ...), custom_call_target="tpu_custom_call" | custom-call | flops 1610612736 | tf_op jit(solution)/shard_map/cond/branch_1_fun/left_products/pallas_call | solution.py:162
  62.2 6.0 %right_products.13 = (f32[512,256]{1,0:T(8,128)S(1)}, f32[512,256]{1,0:T(8,128)}, f32[512,512]{1,0:T(8,128)}) custom-call(s32[2]{0:T(128)S(1)} %get-tuple-element.209.refs_0_, s32[16]{0:T(128)S(1)} %get-tuple-element.208.refs_1_.refs_2_, s32[16]{0:T(128)S(1)} %get-tuple-element.208.refs_1_.refs_2_, s32[4,8]{1,0:T(4,128)S(1)} %get-tuple-element.210.refs_2_.refs_3_, ...), custom_call_target="tpu_custom_call" | custom-call | flops 1610612736 | tf_op jit(solution)/shard_map/cond/branch_1_fun/right_products/pallas_call | solution.py:298
  68.2 2.7 %right_products.12 = f32[512,256]{1,0:T(8,128)S(1)} custom-call(s32[2]{0:T(128)S(1)} %get-tuple-element.209.refs_0_, s32[16]{0:T(128)S(1)} %get-tuple-element.208.refs_1_.refs_2_, s32[16]{0:T(128)S(1)} %get-tuple-element.208.refs_1_.refs_2_, s32[4,8]{1,0:T(4,128)S(1)} %get-tuple-element.210.refs_2_.refs_3_, s32[4,8]{1,0:T(4,128)S(1)} %get-tuple-element.211.refs_3_.refs_4_, ...), custom_call_target="tpu_custom_call" | custom-call | flops 402653184 | tf_op jit(solution)/shard_map/cond/branch_1_fun/right_products/pallas_call | solution.py:298
  70.9 3.9 %collective-permute-done.2 = f32[512,256]{1,0:T(8,128)} collective-permute-done((f32[512,256]{1,0:T(8,128)S(1)}, f32[512,256]{1,0:T(8,128)}, u32[]{:S(2)}, u32[]{:S(2)}) %collective-permute-start.2) | collective-permute-done | bytes 524320 | tf_op jit(solution)/shard_map/cond/branch_1_fun/ppermute | solution.py:433
  75.9 2.4 %collective-permute-start.27 = (f32[512,256]{1,0:T(8,128)S(1)}, f32[512,256]{1,0:T(8,128)S(1)}, u32[]{:S(2)}, u32[]{:S(2)}) collective-permute-start(f32[512,256]{1,0:T(8,128)S(1)} %add.6.refs_0_.refs_9_), channel_id=1, source_target_pairs={{0,4},{1,5},{2,6},{3,7},{4,0},{5,1},{6,2},{7,3},{8,12},{9,13},{10,... | collective-permute-start | bytes 1572872 | tf_op jit(solution)/shard_map/ppermute | solution.py:433
  78.5 25.8 %conditional.4 = (f32[512,256]{1,0:T(8,128)}, s32[1]{0:T(128)}, f32[3,256,256]{2,1,0:T(8,128)S(1)}, f32[256,256]{1,0:T(8,128)S(1)}) conditional(s32[]{:T(128)} %bitcast.4, (f32[512,256]{1,0:T(8,128)S(1)}, s32[2]{0:T(128)S(1)}, s32[16]{0:T(128)S(1)}, s32[4,8]{1,0:T(4,128)S(1)}, s32[4,8]{1,0:T(4,128)S(1)}, ...), branch_computations={%region_3.0_spmd, %region_4.0_spmd, %region_5.0_spmd} | conditional | flops 4026531840 | bytes 6291584 | solution.py:481
  78.5 5.3 %left_products.17.refs_5_ = bf16[2,2,512,512]{3,2,1,0:T(8,128)(2,1)S(1)} custom-call(s32[2]{0:T(128)S(1)} %get-tuple-element.257.refs_0_, s32[16]{0:T(128)S(1)} %get-tuple-element.258.refs_1_, s32[4,8]{1,0:T(4,128)S(1)} %get-tuple-element.260.refs_2_.refs_3_, s32[4,8]{1,0:T(4,128)S(1)} %get-tuple-element.261.refs_3_.refs_4_, ...), custom_call_target="tpu_custom_call" | custom-call | flops 3221225472 | tf_op jit(solution)/shard_map/cond/branch_1_fun/left_products/pallas_call | solution.py:162
  83.9 4.1 %right_products.17 = (s32[1]{0:T(128)}, f32[3,256,256]{2,1,0:T(8,128)S(1)}, f32[256,256]{1,0:T(8,128)S(1)}) custom-call(s32[2]{0:T(128)S(1)} %get-tuple-element.257.refs_0_, s32[16]{0:T(128)S(1)} %get-tuple-element.258.refs_1_, s32[16]{0:T(128)} %get-tuple-element.259.refs_2_, s32[4,8]{1,0:T(4,128)S(1)} %get-tuple-element.260.refs_2_.refs_3_, ...), custom_call_target="tpu_custom_call" | custom-call | flops 805306368 | tf_op jit(solution)/shard_map/cond/branch_1_fun/right_products/pallas_call | solution.py:298
  87.9 16.4 %collective-permute-done.7 = f32[512,256]{1,0:T(8,128)} collective-permute-done((f32[512,256]{1,0:T(8,128)S(1)}, f32[512,256]{1,0:T(8,128)}, u32[]{:S(2)}, u32[]{:S(2)}) %collective-permute-start.7) | collective-permute-done | bytes 524320 | tf_op jit(solution)/shard_map/cond/branch_1_fun/ppermute | solution.py:433
  104.3 1.3 add.7.refs_4_.refs_14_
  105.7 2.4 %collective-permute-start.30 = (f32[512,256]{1,0:T(8,128)S(1)}, f32[512,256]{1,0:T(8,128)}, u32[]{:S(2)}, u32[]{:S(2)}) collective-permute-start(f32[512,256]{1,0:T(8,128)S(1)} %add.7.refs_4_.refs_14_), channel_id=1, source_target_pairs={{0,4},{1,5},{2,6},{3,7},{4,0},{5,1},{6,2},{7,3},{8,12},{9,13},{10,... | collective-permute-start | bytes 1572872 | tf_op jit(solution)/shard_map/ppermute | solution.py:433
  109.0 46.9 %conditional.5 = (f32[3,256,256]{2,1,0:T(8,128)}, f32[256,256]{1,0:T(8,128)S(1)}) conditional(s32[]{:T(128)} %bitcast.9, (f32[3,256,256]{2,1,0:T(8,128)S(1)}, f32[256,256]{1,0:T(8,128)S(1)}) %tuple.66, (f32[3,256,256]{2,1,0:T(8,128)S(1)}, f32[256,256]{1,0:T(8,128)S(1)}) %tuple.66, (f32[3,256,256]{2,1,0:T(8,128)S(1)}, ...), branch_computations={%region_6.0_spmd, %region_7.0_spmd, %region_8.0_spmd, %region_9.0_... | conditional | bytes 4718688 | solution.py:481
  109.1 2.4 %collective-permute-start.14 = (f32[256,256]{1,0:T(8,128)S(1)}, f32[256,256]{1,0:T(8,128)S(1)}, u32[]{:S(2)}, u32[]{:S(2)}) collective-permute-start(f32[256,256]{1,0:T(8,128)S(1)} %get-tuple-element.297), channel_id=1, source_target_pairs={{0,16},{8,24},{16,0},{24,8},{1,17},{9,25},{17,1},{25,9},{2,18},{10... | collective-permute-start | bytes 786440 | tf_op jit(solution)/shard_map/cond/branch_3_fun/ppermute | solution.py:433
  111.4 44.4 %collective-permute-done.14 = f32[256,256]{1,0:T(8,128)S(1)} collective-permute-done((f32[256,256]{1,0:T(8,128)S(1)}, f32[256,256]{1,0:T(8,128)S(1)}, u32[]{:S(2)}, u32[]{:S(2)}) %collective-permute-start.14) | collective-permute-done | bytes 262176 | tf_op jit(solution)/shard_map/cond/branch_3_fun/ppermute | solution.py:433
  155.9 2.3 %wished.1 = f32[2,512,256]{2,1,0:T(8,128)S(1)} custom-call(s32[1]{0:T(128)} %get-tuple-element.367.wish, f32[512,256]{1,0:T(8,128)S(1)} %add.6.refs_0_.refs_9_, f32[512,256]{1,0:T(8,128)S(1)} %collective-permute-done.26.refs_1_.refs_10_, f32[512,256]{1,0:T(8,128)S(1)} %collective-permute-done.27.refs_2_.refs_11_, ...), custom_call_target="tpu_custom_call" | custom-call | tf_op jit(solution)/shard_map/wished/pallas_call | solution.py:417
  158.2 2.6 %collective-permute-done.32.refs_8_.refs_13_ = f32[2,512,256]{2,1,0:T(8,128)S(1)} collective-permute-done((f32[2,512,256]{2,1,0:T(8,128)S(1)}, f32[2,512,256]{2,1,0:T(8,128)S(1)}, u32[]{:S(2)}, u32[]{:S(2)}) %collective-permute-start.32) | collective-permute-done | bytes 1048608 | tf_op jit(solution)/shard_map/ppermute | solution.py:433
  160.9 4.7 %sum_blocks.1 = f32[512,512]{1,0:T(8,128)} custom-call(s32[2]{0:T(128)S(1)} %pad_add_fusion.me.refs_0_, s32[16]{0:T(128)S(1)} %get-tuple-element.340.refs_1_.refs_2_, s32[16]{0:T(128)} %get-tuple-element.349.refs_2_, s32[4,8]{1,0:T(4,128)S(1)} %bitcast.19, s32[4,8]{1,0:T(4,128)S(1)} %copy-done.11, f32[512,512]{1,0:T(8,128)S(1)} %copy-done.9, ...), custom_call_target="tpu_custom_call" | custom-call | tf_op jit(solution)/shard_map/sum_blocks/pallas_call | solution.py:375
  (43 shorter events, 7.0 us)
Async XLA Ops:
  0.0 7.5 %collective-permute-start.18 = (f32[256,256]{1,0:T(8,128)}, f32[256,256]{1,0:T(8,128)S(1)}, u32[]{:S(2)}, u32[]{:S(2)}) collective-permute-start(f32[256,256]{1,0:T(8,128)} %param.22), channel_id=1, source_target_pairs={{0,2},{1,3},{2,0},{3,1},{4,6},{5,7},{6,4},{7,5},{8,10},{9,11},{10,... | collective-permute-start | bytes 786440 | tf_op jit(solution)/shard_map/ppermute | solution.py:433
  0.0 25.5 %collective-permute-start.21 = (f32[512,256]{1,0:T(8,128)}, f32[512,256]{1,0:T(8,128)}, u32[]{:S(2)}, u32[]{:S(2)}) collective-permute-start(f32[512,256]{1,0:T(8,128)} %refs_6_.1), channel_id=1, source_target_pairs={{0,16},{8,24},{16,0},{24,8},{1,17},{9,25},{17,1},{25,9},{2,18},{10... | collective-permute-start | bytes 1572872 | tf_op jit(solution)/shard_map/ppermute | solution.py:433
  2.6 22.9 %collective-permute-start.22 = (f32[512,256]{1,0:T(8,128)}, f32[512,256]{1,0:T(8,128)S(1)}, u32[]{:S(2)}, u32[]{:S(2)}) collective-permute-start(f32[512,256]{1,0:T(8,128)} %refs_6_.1), channel_id=1, source_target_pairs={{0,8},{8,0},{16,24},{24,16},{1,9},{9,1},{17,25},{25,17},{2,10},{10... | collective-permute-start | bytes 1572872 | tf_op jit(solution)/shard_map/ppermute | solution.py:433
  3.9 6.6 %collective-permute-start.19 = (f32[256,256]{1,0:T(8,128)}, f32[256,256]{1,0:T(8,128)S(1)}, u32[]{:S(2)}, u32[]{:S(2)}) collective-permute-start(f32[256,256]{1,0:T(8,128)} %param.22), channel_id=1, source_target_pairs={{0,4},{1,5},{2,6},{3,7},{4,0},{5,1},{6,2},{7,3},{8,12},{9,13},{10,... | collective-permute-start | bytes 786440 | tf_op jit(solution)/shard_map/ppermute | solution.py:433
  7.5 8.6 %collective-permute-start.20 = (f32[256,256]{1,0:T(8,128)S(1)}, f32[256,256]{1,0:T(8,128)S(1)}, u32[]{:S(2)}, u32[]{:S(2)}) collective-permute-start(f32[256,256]{1,0:T(8,128)S(1)} %collective-permute-done.18), channel_id=1, source_target_pairs={{0,4},{1,5},{2,6},{3,7},{4,0},{5,1},{6,2},{7,3},{8,12},{9,13},{10,... | collective-permute-start | bytes 786440 | tf_op jit(solution)/shard_map/ppermute | solution.py:433
  25.5 22.9 %copy-start.5 = (f32[512,256]{1,0:T(8,128)}, f32[512,256]{1,0:T(8,128)S(1)}, u32[]{:S(2)}) copy-start(f32[512,256]{1,0:T(8,128)S(1)} %collective-permute-done.22.refs_7_) | copy-start | bytes 1572868
  26.7 5.2 %collective-permute-start.23 = (f32[4,256,256]{2,1,0:T(8,128)S(1)}, f32[4,256,256]{2,1,0:T(8,128)S(1)}, u32[]{:S(2)}, u32[]{:S(2)}) collective-permute-start(f32[4,256,256]{2,1,0:T(8,128)S(1)} %pad_maximum_fusion.refs_5_), channel_id=1, source_target_pairs={{0,1},{1,0},{2,3},{3,2},{4,5},{5,4},{6,7},{7,6},{8,9},{9,8},{10,11... | collective-permute-start | bytes 3145736 | tf_op jit(solution)/shard_map/ppermute | solution.py:433
  28.5 7.4 %collective-permute-start.24 = (f32[512,256]{1,0:T(8,128)}, f32[512,256]{1,0:T(8,128)}, u32[]{:S(2)}, u32[]{:S(2)}) collective-permute-start(f32[512,256]{1,0:T(8,128)} %refs_6_.1), channel_id=1, source_target_pairs={{8,16},{16,8},{9,17},{17,9},{10,18},{18,10},{11,19},{19,11},{12,20... | collective-permute-start | bytes 1572872 | tf_op jit(solution)/shard_map/ppermute | solution.py:440
  29.9 15.7 %collective-permute-start.25 = (f32[512,256]{1,0:T(8,128)}, f32[512,256]{1,0:T(8,128)}, u32[]{:S(2)}, u32[]{:S(2)}) collective-permute-start(f32[512,256]{1,0:T(8,128)} %collective-permute-done.21.refs_8_), channel_id=1, source_target_pairs={{8,0},{16,24},{9,1},{17,25},{10,2},{18,26},{11,3},{19,27},{12,4},{... | collective-permute-start | bytes 1572872 | tf_op jit(solution)/shard_map/ppermute | solution.py:449
  31.9 13.8 %copy-start.1 = (f32[512,256]{1,0:T(8,128)S(1)}, f32[512,256]{1,0:T(8,128)}, u32[]{:S(2)}) copy-start(f32[512,256]{1,0:T(8,128)} %refs_6_.1) | copy-start | bytes 1572868
  31.9 13.8 %copy-start.10 = (s32[8,4]{0,1:T(4,128)S(1)}, s32[8,4]{0,1:T(4,128)}, u32[]{:S(2)}) copy-start(s32[8,4]{0,1:T(4,128)} %param.24) | copy-start | bytes 388
  31.9 13.8 %copy-start.11 = (s32[4,8]{1,0:T(4,128)S(1)}, s32[4,8]{1,0:T(4,128)}, u32[]{:S(2)}) copy-start(s32[4,8]{1,0:T(4,128)} %refs_4_.5) | copy-start | bytes 388
  31.9 16.5 %copy-start = (f32[4,256,256]{2,1,0:T(8,128)}, f32[4,256,256]{2,1,0:T(8,128)S(1)}, u32[]{:S(2)}) copy-start(f32[4,256,256]{2,1,0:T(8,128)S(1)} %collective-permute-done.23.refs_6_) | copy-start | bytes 3145732
  48.4 22.4 %collective-permute-start.3 = (s32[16]{0:T(128)S(1)}, s32[16]{0:T(128)}, u32[]{:S(2)}, u32[]{:S(2)}) collective-permute-start(s32[16]{0:T(128)S(1)} %get-tuple-element.208.refs_1_.refs_2_), channel_id=1, source_target_pairs={{0,16},{8,24},{16,0},{24,8},{1,17},{9,25},{17,1},{25,9},{2,18},{10... | collective-permute-start | bytes 200 | tf_op jit(solution)/shard_map/cond/branch_1_fun/ppermute | solution.py:433
  49.6 25.1 %collective-permute-start.2 = (f32[512,256]{1,0:T(8,128)S(1)}, f32[512,256]{1,0:T(8,128)}, u32[]{:S(2)}, u32[]{:S(2)}) collective-permute-start(f32[512,256]{1,0:T(8,128)S(1)} %get-tuple-element.207), channel_id=1, source_target_pairs={{0,16},{8,24},{16,0},{24,8},{1,17},{9,25},{17,1},{25,9},{2,18},{10... | collective-permute-start | bytes 1572872 | tf_op jit(solution)/shard_map/cond/branch_1_fun/ppermute | solution.py:433
  75.8 28.5 %collective-permute-start.26 = (f32[512,256]{1,0:T(8,128)S(1)}, f32[512,256]{1,0:T(8,128)S(1)}, u32[]{:S(2)}, u32[]{:S(2)}) collective-permute-start(f32[512,256]{1,0:T(8,128)S(1)} %add.6.refs_0_.refs_9_), channel_id=1, source_target_pairs={{0,2},{1,3},{2,0},{3,1},{4,6},{5,7},{6,4},{7,5},{8,10},{9,11},{10,... | collective-permute-start | bytes 1572872 | tf_op jit(solution)/shard_map/ppermute | solution.py:433
  75.9 28.4 %collective-permute-start.27 = (f32[512,256]{1,0:T(8,128)S(1)}, f32[512,256]{1,0:T(8,128)S(1)}, u32[]{:S(2)}, u32[]{:S(2)}) collective-permute-start(f32[512,256]{1,0:T(8,128)S(1)} %add.6.refs_0_.refs_9_), channel_id=1, source_target_pairs={{0,4},{1,5},{2,6},{3,7},{4,0},{5,1},{6,2},{7,3},{8,12},{9,13},{10,... | collective-permute-start | bytes 1572872 | tf_op jit(solution)/shard_map/ppermute | solution.py:433
  78.3 26.0 %collective-permute-start.28 = (f32[512,256]{1,0:T(8,128)S(1)}, f32[512,256]{1,0:T(8,128)S(1)}, u32[]{:S(2)}, u32[]{:S(2)}) collective-permute-start(f32[512,256]{1,0:T(8,128)S(1)} %add.6.refs_0_.refs_9_), channel_id=1, source_target_pairs={{0,6},{1,7},{2,4},{3,5},{4,2},{5,3},{6,0},{7,1},{8,14},{9,15},{10,... | collective-permute-start | bytes 1572872 | tf_op jit(solution)/shard_map/ppermute | solution.py:433
  78.5 25.8 %collective-permute-start.7 = (f32[512,256]{1,0:T(8,128)S(1)}, f32[512,256]{1,0:T(8,128)}, u32[]{:S(2)}, u32[]{:S(2)}) collective-permute-start(f32[512,256]{1,0:T(8,128)S(1)} %get-tuple-element.256), channel_id=1, source_target_pairs={{0,16},{8,24},{16,0},{24,8},{1,17},{9,25},{17,1},{25,9},{2,18},{10... | collective-permute-start | bytes 1572872 | tf_op jit(solution)/shard_map/cond/branch_1_fun/ppermute | solution.py:433
  78.5 5.3 %copy-start.3 = (f32[512,256]{1,0:T(8,128)S(1)}, f32[512,256]{1,0:T(8,128)}, u32[]{:S(2)}) copy-start(f32[512,256]{1,0:T(8,128)} %get-tuple-element.265.refs_6_) | copy-start | bytes 1572868 | tf_op jit(solution)/shard_map/cond
  78.5 5.3 %copy-start.7 = (f32[512,256]{1,0:T(8,128)S(1)}, f32[512,256]{1,0:T(8,128)}, u32[]{:S(2)}) copy-start(f32[512,256]{1,0:T(8,128)} %get-tuple-element.266.refs_7_) | copy-start | bytes 1572868 | tf_op jit(solution)/shard_map/cond
  105.6 50.2 %collective-permute-start.29 = (f32[512,256]{1,0:T(8,128)S(1)}, f32[512,256]{1,0:T(8,128)S(1)}, u32[]{:S(2)}, u32[]{:S(2)}) collective-permute-start(f32[512,256]{1,0:T(8,128)S(1)} %add.7.refs_4_.refs_14_), channel_id=1, source_target_pairs={{0,2},{1,3},{2,0},{3,1},{4,6},{5,7},{6,4},{7,5},{8,10},{9,11},{10,... | collective-permute-start | bytes 1572872 | tf_op jit(solution)/shard_map/ppermute | solution.py:433
  105.7 50.2 %collective-permute-start.30 = (f32[512,256]{1,0:T(8,128)S(1)}, f32[512,256]{1,0:T(8,128)}, u32[]{:S(2)}, u32[]{:S(2)}) collective-permute-start(f32[512,256]{1,0:T(8,128)S(1)} %add.7.refs_4_.refs_14_), channel_id=1, source_target_pairs={{0,4},{1,5},{2,6},{3,7},{4,0},{5,1},{6,2},{7,3},{8,12},{9,13},{10,... | collective-permute-start | bytes 1572872 | tf_op jit(solution)/shard_map/ppermute | solution.py:433
  108.1 47.8 %collective-permute-start.31 = (f32[512,256]{1,0:T(8,128)S(1)}, f32[512,256]{1,0:T(8,128)}, u32[]{:S(2)}, u32[]{:S(2)}) collective-permute-start(f32[512,256]{1,0:T(8,128)S(1)} %add.7.refs_4_.refs_14_), channel_id=1, source_target_pairs={{0,6},{1,7},{2,4},{3,5},{4,2},{5,3},{6,0},{7,1},{8,14},{9,15},{10,... | collective-permute-start | bytes 1572872 | tf_op jit(solution)/shard_map/ppermute | solution.py:433
  109.0 46.8 %collective-permute-start.13 = (f32[3,256,256]{2,1,0:T(8,128)S(1)}, f32[3,256,256]{2,1,0:T(8,128)}, u32[]{:S(2)}, u32[]{:S(2)}) collective-permute-start(f32[3,256,256]{2,1,0:T(8,128)S(1)} %get-tuple-element.296), channel_id=1, source_target_pairs={{0,16},{8,24},{16,0},{24,8},{1,17},{9,25},{17,1},{25,9},{2,18},{10... | collective-permute-start | bytes 2359304 | tf_op jit(solution)/shard_map/cond/branch_3_fun/ppermute | solution.py:433
  109.1 46.7 %collective-permute-start.14 = (f32[256,256]{1,0:T(8,128)S(1)}, f32[256,256]{1,0:T(8,128)S(1)}, u32[]{:S(2)}, u32[]{:S(2)}) collective-permute-start(f32[256,256]{1,0:T(8,128)S(1)} %get-tuple-element.297), channel_id=1, source_target_pairs={{0,16},{8,24},{16,0},{24,8},{1,17},{9,25},{17,1},{25,9},{2,18},{10... | collective-permute-start | bytes 786440 | tf_op jit(solution)/shard_map/cond/branch_3_fun/ppermute | solution.py:433
  155.8 5.0 %copy-start.9 = (f32[512,512]{1,0:T(8,128)S(1)}, f32[512,512]{1,0:T(8,128)}, u32[]{:S(2)}) copy-start(f32[512,512]{1,0:T(8,128)} %get-tuple-element.350.refs_5_) | copy-start | bytes 3145732
  158.1 2.7 %collective-permute-start.32 = (f32[2,512,256]{2,1,0:T(8,128)S(1)}, f32[2,512,256]{2,1,0:T(8,128)S(1)}, u32[]{:S(2)}, u32[]{:S(2)}) collective-permute-start(f32[2,512,256]{2,1,0:T(8,128)S(1)} %wished.1), channel_id=1, source_target_pairs={{0,1},{1,0},{2,3},{3,2},{4,5},{5,4},{6,7},{7,6},{8,9},{9,8},{10,11... | collective-permute-start | bytes 3145736 | tf_op jit(solution)/shard_map/ppermute | solution.py:433
